TPU v7x, 512 devices: a whole 4x4x16 slice. The times are simulated.
512 devices in a mesh: clip: 32 (over x_hi, z), frame: 16 (over y, x_lo, core).
Axes of the slice: x: 4 (x_hi: 2, x_lo: 2; x = x_hi * 2 + x_lo), y: 4, z: 16, core: 2. Of those that a mesh axis runs over, the one named last changes fastest.
Arguments:
- clips: bfloat16 [32, 16, 16, 32, 256], P('clip', 'frame'), may hold values from -25 to 25, as said below
- cotangent: bfloat16 [32, 16, 16, 32, 256], P('clip', 'frame'), may hold values from -25 to 25
- norm_gain: float32 [256], replicated, may hold values from 0.25 to 1.75
- norm_shift: float32 [256], replicated, may hold values from -3 to 3
- w_spatial: bfloat16 [3, 3, 256, 256], replicated, may hold values from -0.125 to 0.125
- w_time: bfloat16 [3, 256, 256], replicated, may hold values from -0.21875 to 0.21875
Outputs:
- result_video: bfloat16 [32, 16, 16, 32, 256], P('clip', 'frame')
- input_grad: bfloat16 [32, 16, 16, 32, 256], P('clip', 'frame')
- spatial_grad: bfloat16 [3, 3, 256, 256], P(None, None, 'frame')
- time_grad: bfloat16 [3, 256, 256], P(None, 'frame')
Inputs may be any that keep to these rules, and one draw needn't show every extreme that they name: `clips`: input activations.
All inputs are finite; a program needn't handle non-finite values.
Results may differ from a plain program's by a relative error of at most 0.0029.
Values may be sent and summed in bfloat16 or wider, within the bound.
A program may use at most 64 MiB of HBM per device.

v0:
```python
import math

import jax
import jax.numpy as jnp
from jax import lax
from jax.sharding import PartitionSpec as P

GROUPS = 32


epsilon = 1e-05


def group_sums(values, groups):
    return values.reshape(groups, -1).sum(axis=1)


def spread_groups(values, channels):
    return jnp.repeat(values, channels // values.shape[0])


def spatial_conv(hidden, weights):
    row_count, col_count, channels = (hidden.shape[1], hidden.shape[2], hidden.shape[3])
    padded = jnp.pad(hidden, ((0, 0), (1, 1), (1, 1), (0, 0)))
    running = jnp.zeros((hidden.shape[0] * row_count * col_count, weights.shape[-1]), jnp.float32)
    for row_tap in range(3):
        for col_tap in range(3):
            window = padded[
                :, row_tap : row_tap + row_count, col_tap : col_tap + col_count, :
            ].reshape(-1, channels)
            running = running + jnp.dot(
                window, weights[row_tap, col_tap], preferred_element_type=jnp.float32
            )
    return running.reshape(hidden.shape[:-1] + (weights.shape[-1],))


def spatial_weights(hidden, gradient):
    row_count, col_count, channels = (hidden.shape[1], hidden.shape[2], hidden.shape[3])
    padded = jnp.pad(hidden, ((0, 0), (1, 1), (1, 1), (0, 0)))
    flat_grad = gradient.reshape(-1, gradient.shape[-1])
    rows_out = []
    for row_tap in range(3):
        cols_out = []
        for col_tap in range(3):
            window = padded[
                :, row_tap : row_tap + row_count, col_tap : col_tap + col_count, :
            ].reshape(-1, channels)
            cols_out.append(jnp.dot(window.T, flat_grad, preferred_element_type=jnp.float32))
        rows_out.append(jnp.stack(cols_out))
    return jnp.stack(rows_out)


def causal_conv(sequence, w_time):
    frames, channels = (sequence.shape[0], sequence.shape[-1])
    padded = jnp.pad(sequence, ((2, 0),) + ((0, 0),) * (sequence.ndim - 1))
    running = jnp.zeros((sequence.size // channels, channels), jnp.float32)
    for offset in range(3):
        running = running + jnp.dot(
            padded[2 - offset : 2 - offset + frames].reshape(-1, channels),
            w_time[offset],
            preferred_element_type=jnp.float32,
        )
    return running.reshape(sequence.shape)


def causal_back(gradient, w_time):
    frames, channels = (gradient.shape[0], gradient.shape[-1])
    padded = jnp.pad(gradient, ((0, 2),) + ((0, 0),) * (gradient.ndim - 1))
    running = jnp.zeros((gradient.size // channels, channels), jnp.float32)
    for offset in range(3):
        running = running + jnp.dot(
            padded[offset : offset + frames].reshape(-1, channels),
            w_time[offset].T,
            preferred_element_type=jnp.float32,
        )
    return running.reshape(gradient.shape)


def causal_weights(sequence, gradient):
    frames, channels = (sequence.shape[0], sequence.shape[-1])
    padded = jnp.pad(sequence, ((2, 0),) + ((0, 0),) * (sequence.ndim - 1))
    flat_grad = gradient.reshape(-1, channels)
    return jnp.stack(
        [
            jnp.dot(
                padded[2 - offset : 2 - offset + frames].reshape(-1, channels).T,
                flat_grad,
                preferred_element_type=jnp.float32,
            )
            for offset in range(3)
        ]
    )


def per_device(clips, cotangent, norm_gain, norm_shift, w_spatial, w_time):
    frame_count = lax.axis_size("frame")
    clip_count = lax.axis_size("clip")
    video_frame = clips[0]
    grad_frame = cotangent[0]
    row_count, col_count, channels = (
        video_frame.shape[1],
        video_frame.shape[2],
        video_frame.shape[3],
    )
    members = frame_count * row_count * col_count * (channels // GROUPS)
    values = video_frame.astype(jnp.float32)
    value_sum = lax.psum(group_sums(jnp.sum(values, axis=(0, 1, 2)), GROUPS), "frame")
    center = value_sum / members
    centered = values - spread_groups(center, channels)
    square_sum = lax.psum(group_sums(jnp.sum(centered * centered, axis=(0, 1, 2)), GROUPS), "frame")
    variance = square_sum / members
    inv_std = lax.rsqrt(variance + epsilon)
    normed = centered * spread_groups(inv_std, channels)
    activation = normed * norm_gain + norm_shift
    hidden = jax.nn.silu(activation).astype(jnp.bfloat16)
    mixed_frame = spatial_conv(hidden, w_spatial).astype(jnp.bfloat16)
    mixed_band, grad_band = (
        lax.all_to_all(mixed_frame[None], "frame", split_axis=2, concat_axis=1, tiled=True),
        lax.all_to_all(cotangent, "frame", split_axis=2, concat_axis=1, tiled=True),
    )
    band_out = causal_conv(mixed_band[0], w_time).astype(jnp.bfloat16)
    back_band = causal_back(grad_band[0], w_time).astype(jnp.bfloat16)
    time_part = causal_weights(mixed_band[0], grad_band[0])
    temporal, mixed_home = (
        lax.all_to_all(band_out[None], "frame", split_axis=1, concat_axis=2, tiled=True),
        lax.all_to_all(back_band[None], "frame", split_axis=1, concat_axis=2, tiled=True),
    )
    mixed_grad = mixed_home[0]
    result_video = (clips.astype(jnp.float32) + temporal.astype(jnp.float32)).astype(jnp.bfloat16)
    spatial_part = spatial_weights(hidden, mixed_grad)
    flipped = jnp.swapaxes(w_spatial[::-1, ::-1], 2, 3)
    hidden_grad = spatial_conv(mixed_grad, flipped)
    sigmoid_act = jax.nn.sigmoid(activation)
    act_grad = hidden_grad * sigmoid_act * (1.0 + activation * (1.0 - sigmoid_act))
    normed_grad = act_grad * norm_gain
    first_sum, second_sum = lax.psum(
        (
            group_sums(jnp.sum(normed_grad, axis=(0, 1, 2)), GROUPS),
            group_sums(jnp.sum(normed_grad * normed, axis=(0, 1, 2)), GROUPS),
        ),
        "frame",
    )
    input_grad = grad_frame.astype(jnp.float32) + spread_groups(inv_std, channels) * (
        normed_grad
        - spread_groups(first_sum / members, channels)
        - normed * spread_groups(second_sum / members, channels)
    )
    stacked = jnp.concatenate([spatial_part.reshape(9, channels, channels), time_part], axis=0)
    grad_share = lax.psum_scatter(stacked, "frame", scatter_dimension=1, tiled=True)
    grad_share = lax.psum(grad_share, "clip")
    grad_scale = 1.0 / math.sqrt(clip_count * frame_count * row_count * col_count)
    grad_share = grad_share * grad_scale
    spatial_out = grad_share[:9].reshape(3, 3, grad_share.shape[1], channels).astype(jnp.bfloat16)
    time_out = grad_share[9:].astype(jnp.bfloat16)
    return (result_video, input_grad.astype(jnp.bfloat16)[None], spatial_out, time_out)


def solution(mesh):
    placed = (
        P("clip", "frame", None, None, None),
        P("clip", "frame", None, None, None),
        P(),
        P(),
        P(),
        P(),
    )
    return jax.shard_map(
        per_device,
        mesh=mesh,
        in_specs=placed,
        out_specs=(
            P("clip", "frame", None, None, None),
            P("clip", "frame", None, None, None),
            P(None, None, "frame", None),
            P(None, "frame", None),
        ),
        check_vma=False,
    )
```

profile of v0, /device:TPU:16, one launch (start us, length us, event | category | flops | bytes accessed | tf_op | source)
XLA Modules:
  0.0 527.6 jit_solution(11038506905976836317)
XLA Ops:
  7.2 9.2 %all-to-all-start.2 = ((bf16[1,1,16,32,256]{4,3,1,0,2:T(8,128)(2,1)}), bf16[1,1,16,32,256]{4,3,1,0,2:T(8,128)(2,1)S(1)}, u32[]{:S(2)}, u32[]{:S(2)}) async-start(bf16[1,1,16,32,256]{4,3,1,0,2:T(8,128)(2,1)} %bitcast.264), calls=%async_computation.2 | async-start | bytes 524288 | tf_op jit(solution)/shard_map/all_to_all | solution.py:119
  16.4 1.0 convert_reduce_fusion
  17.7 23.5 %psum.35 = f32[32]{0:T(128)S(1)} all-reduce(f32[32]{0:T(128)S(1)} %reduce_sum.73), channel_id=1, replica_groups=mesh['clip'=32,'frame'=16] {'frame'}, use_global_device_ids=true, to_apply=%region_2.0 | all-reduce | flops 32 | bytes 256 | tf_op jit(solution)/shard_map/psum | solution.py:107
  41.3 1.1 multiply_reduce_fusion.1
  42.6 22.3 %psum.36 = f32[32]{0:T(128)S(1)} all-reduce(f32[32]{0:T(128)S(1)} %reduce_sum.75), channel_id=1, replica_groups=mesh['clip'=32,'frame'=16] {'frame'}, use_global_device_ids=true, to_apply=%region_5.0 | all-reduce | flops 32 | bytes 256 | tf_op jit(solution)/shard_map/psum | solution.py:110
  66.7 1.2 reverse_bitcast_fusion
  68.4 1.1 convolution_add_fusion.18
  69.5 1.2 fusion.12
  71.9 15.8 %all-to-all-start.3 = ((bf16[1,16,1,32,256]{4,3,2,0,1:T(8,128)(2,1)}), bf16[1,16,1,32,256]{4,3,2,0,1:T(8,128)(2,1)S(1)}, u32[]{:S(2)}, u32[]{:S(2)}) async-start(bf16[1,16,1,32,256]{4,3,2,0,1:T(8,128)(2,1)} %bitcast.266), calls=%async_computation.3 | async-start | bytes 524288 | tf_op jit(solution)/shard_map/all_to_all | solution.py:126
  87.7 2.2 convolution_add_fusion.17
  89.9 3.3 all-to-all-done.3
  93.2 1.9 convolution_bitcast_fusion.8
  95.1 1.9 convolution_bitcast_fusion.9
  97.0 1.9 convolution_bitcast_fusion.10
  103.3 1.2 fusion.41
  104.9 23.7 %all-reduce.4 = (f32[32]{0:T(128)S(1)}, f32[32]{0:T(128)S(1)}) all-reduce(f32[32]{0:T(128)S(1)} %reduce_sum.79, f32[32]{0:T(128)S(1)} %reduce_sum.77), channel_id=1, replica_groups=mesh['clip'=32,'frame'=16] {'frame'}, use_global_device_ids=true, to_apply=%region_11.12 | all-reduce | flops 64 | bytes 512 | tf_op jit(solution)/shard_map/psum | solution.py:136
  129.0 2.3 add_convert_fusion
  136.5 10.4 %all-to-all-start = ((bf16[1,1,16,32,256]{4,3,1,0,2:T(8,128)(2,1)}), bf16[1,1,16,32,256]{4,3,1,0,2:T(8,128)(2,1)S(1)}, u32[]{:S(2)}, u32[]{:S(2)}) async-start(bf16[1,1,16,32,256]{4,3,1,0,2:T(8,128)(2,1)} %bitcast.265), calls=%async_computation | async-start | bytes 524288 | tf_op jit(solution)/shard_map/all_to_all | solution.py:118
  146.9 1.0 maximum_bitcast_fusion.2
  149.3 3.0 all-to-all-done
  153.2 2.0 pad_maximum_fusion
  157.7 6.1 %all-to-all-start.1 = ((bf16[1,16,1,32,256]{4,3,2,0,1:T(8,128)(2,1)}), bf16[1,16,1,32,256]{4,3,2,0,1:T(8,128)(2,1)S(1)}, u32[]{:S(2)}, u32[]{:S(2)}) async-start(bf16[1,16,1,32,256]{4,3,2,0,1:T(8,128)(2,1)} %bitcast.29), calls=%async_computation.1 | async-start | bytes 524288 | tf_op jit(solution)/shard_map/all_to_all | solution.py:125
  163.8 57.4 %reduce-scatter.2.cloned.1.call-done = f32[12,16,256]{2,1,0:T(8,128)} async-done(((f32[12,256,256]{2,1,0:T(8,128)}), f32[12,16,256]{2,1,0:T(8,128)}) %reduce-scatter.2.cloned.1.call-update) | async-done | bytes 196624 | tf_op jit(solution)/shard_map/reduce_scatter | solution.py:149
  222.0 296.5 %all-reduce.7.cloned.1.call-done = f32[12,16,256]{2,1,0:T(8,128)} async-done(((f32[12,16,256]{2,1,0:T(8,128)}), f32[12,16,256]{2,1,0:T(8,128)}) %all-reduce.7.cloned.1.call-update) | async-done | bytes 196624 | tf_op jit(solution)/shard_map/psum | solution.py:150
  (102 shorter events, 21.9 us)
Async XLA Ops:
  7.2 57.9 %copy-start = (bf16[1,1,16,32,256]{4,3,2,1,0:T(8,128)(2,1)S(1)}, bf16[1,1,16,32,256]{4,3,2,1,0:T(8,128)(2,1)}, u32[]{:S(2)}) copy-start(bf16[1,1,16,32,256]{4,3,2,1,0:T(8,128)(2,1)} %param.6) | copy-start | bytes 786436
  7.2 57.9 %copy-start.16 = (f32[256]{0:T(256)S(1)}, f32[256]{0:T(256)}, u32[]{:S(2)}) copy-start(f32[256]{0:T(256)} %param.9) | copy-start | bytes 3076
  7.2 57.9 %copy-start.17 = (f32[256]{0:T(256)S(1)}, f32[256]{0:T(256)}, u32[]{:S(2)}) copy-start(f32[256]{0:T(256)} %param.8) | copy-start | bytes 3076
  7.2 62.2 %all-to-all-start.2 = ((bf16[1,1,16,32,256]{4,3,1,0,2:T(8,128)(2,1)}), bf16[1,1,16,32,256]{4,3,1,0,2:T(8,128)(2,1)S(1)}, u32[]{:S(2)}, u32[]{:S(2)}) async-start(bf16[1,1,16,32,256]{4,3,1,0,2:T(8,128)(2,1)} %bitcast.264), calls=%async_computation.2 | async-start | bytes 524288 | tf_op jit(solution)/shard_map/all_to_all | solution.py:119
  65.3 1.4 copy-start.1
  66.7 1.7 copy-start.3
  66.7 1.7 copy-start.4
  69.4 1.3 copy-start.8
  71.9 21.2 %all-to-all-start.3 = ((bf16[1,16,1,32,256]{4,3,2,0,1:T(8,128)(2,1)}), bf16[1,16,1,32,256]{4,3,2,0,1:T(8,128)(2,1)S(1)}, u32[]{:S(2)}, u32[]{:S(2)}) async-start(bf16[1,16,1,32,256]{4,3,2,0,1:T(8,128)(2,1)} %bitcast.266), calls=%async_computation.3 | async-start | bytes 524288 | tf_op jit(solution)/shard_map/all_to_all | solution.py:126
  99.9 1.3 copy-start.2
  128.9 3.2 copy-start.7
  134.6 12.3 %copy-start.15 = (f32[1,256,256]{2,1,0:T(8,128)S(1)}, f32[1,256,256]{2,1,0:T(8,128)}, u32[]{:S(2)}) copy-start(f32[1,256,256]{2,1,0:T(8,128)} %convolution_bitcast_fusion.4) | copy-start | bytes 786436
  136.5 11.4 %copy-start.12 = (f32[1,256,256]{2,1,0:T(8,128)S(1)}, f32[1,256,256]{2,1,0:T(8,128)}, u32[]{:S(2)}) copy-start(f32[1,256,256]{2,1,0:T(8,128)} %convolution_bitcast_fusion.8) | copy-start | bytes 786436
  136.5 11.4 %copy-start.14 = (f32[1,256,256]{2,1,0:T(8,128)S(1)}, f32[1,256,256]{2,1,0:T(8,128)}, u32[]{:S(2)}) copy-start(f32[1,256,256]{2,1,0:T(8,128)} %convolution_bitcast_fusion.7) | copy-start | bytes 786436
  136.5 15.8 %all-to-all-start = ((bf16[1,1,16,32,256]{4,3,1,0,2:T(8,128)(2,1)}), bf16[1,1,16,32,256]{4,3,1,0,2:T(8,128)(2,1)S(1)}, u32[]{:S(2)}, u32[]{:S(2)}) async-start(bf16[1,1,16,32,256]{4,3,1,0,2:T(8,128)(2,1)} %bitcast.265), calls=%async_computation | async-start | bytes 524288 | tf_op jit(solution)/shard_map/all_to_all | solution.py:118
  146.9 74.3 %reduce-scatter.2.cloned.1.call-start = ((), (), s32[]{:S(2)}) async-start(), calls=%async_computation.5 | async-start | bytes 3342336 | tf_op jit(solution)/shard_map/reduce_scatter | solution.py:149
  148.0 1.0 copy-start.10
  148.0 1.0 copy-start.11
  148.0 1.1 copy-start.13
  152.4 0.8 copy-start.5
  155.3 1.0 copy-start.9
  155.3 1.2 copy-start.6
  157.7 63.6 %all-to-all-start.1 = ((bf16[1,16,1,32,256]{4,3,2,0,1:T(8,128)(2,1)}), bf16[1,16,1,32,256]{4,3,2,0,1:T(8,128)(2,1)S(1)}, u32[]{:S(2)}, u32[]{:S(2)}) async-start(bf16[1,16,1,32,256]{4,3,2,0,1:T(8,128)(2,1)} %bitcast.29), calls=%async_computation.1 | async-start | bytes 524288 | tf_op jit(solution)/shard_map/all_to_all | solution.py:125
  163.8 354.8 %all-reduce.7.cloned.1.call-start = ((), (), s32[]{:S(2)}) async-start(), calls=%async_computation.6 | async-start | bytes 393216 | tf_op jit(solution)/shard_map/psum | solution.py:150
Sparse Core Ops, SparseCore 0:
  155.4 65.7 reduce-scatter.1
  224.1 294.3 all-reduce.6
where the time goes:
time: 529 us; the launch traced here: 528 us
  waiting for transfers between devices  360 us (68%)
  blocking collectives  69.5 us (13%)
  starting transfers between devices  41.5 us (8%)
  matrix products  23.5 us (4%)
  between operations  14.5 us (3%)
  other arithmetic  10.1 us (2%)
  local copies, waits for them, and re-layouts  8.18 us (2%)
    psum x1, waiting for transfers between devices, per_device(): grad_share = lax.psum(grad_share, 'clip')  296 us
    reduce_scatter x1, waiting for transfers between devices, per_device(): lax.psum_scatter(stacked, 'frame', scatter_dimension=1, tiled=True)  57.4 us
    psum x1, blocking collectives, per_device(): lax.psum((group_sums(jnp.sum(normed_grad, axis=(0, 1, 2)), GROUPS), group...  23.7 us
    psum x1, blocking collectives, per_device(): lax.psum(group_sums(jnp.sum(values, axis=(0, 1, 2)), GROUPS), 'frame')  23.5 us
    psum x1, blocking collectives, per_device(): lax.psum(group_sums(jnp.sum(centered * centered, axis=(0, 1, 2)), GROUPS)...  22.3 us
    all_to_all x1, starting transfers between devices, per_device(): lax.all_to_all(back_band[None], 'frame', split_axis=1, concat_axis=2, til...  15.8 us
  transfers between devices with their start and end apart: 6, of which 4 were waited for; matrix products, arithmetic and copies ran while one was open for 2% of the time, Pallas kernels for 0%

commit v1 on v0

v1 whole, which is shorter than its diff:
```python
import functools
import math

import jax
import jax.numpy as jnp
from jax import lax
from jax.experimental import pallas as pl
from jax.experimental.pallas import tpu as pltpu
from jax.sharding import PartitionSpec as P

GROUPS = 32
EPSILON = 1e-05
MESH = pl.DeviceIdType.MESH
F32 = jnp.float32
BF16 = jnp.bfloat16

ROWS, COLS, C = 16, 32, 256
POS = ROWS * COLS
PAD = COLS
TAPS = 12
CHUNKS = 4
PIECE = POS // CHUNKS

ZS, XH, CHIPS = 16, 2, 8
FRAMES = 2 * CHIPS


def dot(a, b):
    return jnp.dot(a, b, preferred_element_type=F32)


def remote(src, dst, send_sem, recv_sem, clip, frame):
    return pltpu.make_async_remote_copy(
        src_ref=src,
        dst_ref=dst,
        send_sem=send_sem,
        recv_sem=recv_sem,
        device_id=(clip, frame),
        device_id_type=MESH,
    )


def wait_for(ref, sem):
    pltpu.make_async_copy(ref, ref, sem).wait()


def loop(count, body):
    def step(i, carry):
        body(i)
        return carry

    lax.fori_loop(0, count, step, 0)


def group_spread(row):
    lane = lax.broadcasted_iota(jnp.int32, row.shape, 1)
    for bit in (1, 2, 4):
        up = pltpu.roll(row, bit, 1)
        down = pltpu.roll(row, row.shape[1] - bit, 1)
        row = row + jnp.where((lane & bit) != 0, up, down)
    return row


def shifted(values, by, column):
    if by == 0:
        return values
    rolled = pltpu.roll(values, (-by) % values.shape[0], 0)
    edge = 0 if by < 0 else COLS - 1
    return jnp.where(column == edge, 0.0, rolled)


def by_parity(columns):
    strips = columns.reshape(8, 2, 16, columns.shape[1])
    return (
        strips[:, 0].reshape(128, columns.shape[1]),
        strips[:, 1].reshape(128, columns.shape[1]),
    )


def kernel(
    clips, cot, gain, shift, w_space, w_time,
    result_out, grad_out, space_out, time_out,
    clips_v, cot4, w_space_v, w_time_v, w_space_t, w_time_t,
    hcat, mgcat, act_s, ng_s, h_t, h_tx, m_t, m_tx, mixed_own, mixed_halo, mixed_sib,
    stat_tx, stat_rx, mean_tx, mean_rx,
    rs_tx_a, rs_rx_a, rs_tx_b, rs_rx_b, z_tx, z_rx, fin_tx, gathered,
    local_sem, send_sem, recv_sem, piece_sem,
):
    clip = lax.axis_index("clip")
    frame = lax.axis_index("frame")
    xh, z = clip // ZS, lax.rem(clip, ZS)
    q, core = frame // 2, lax.rem(frame, 2)
    sibling = frame + 1 - 2 * core
    members = FRAMES * POS * (C // GROUPS)

    copies = [
        pltpu.make_async_copy(clips, clips_v, local_sem.at[0]),
        pltpu.make_async_copy(w_time, w_time_v, local_sem.at[1]),
        pltpu.make_async_copy(w_space, w_space_v, local_sem.at[2]),
        pltpu.make_async_copy(cot, cot4.at[core], local_sem.at[3]),
    ]
    for copy in copies:
        copy.start()

    barrier = pltpu.get_barrier_semaphore()

    def greet(clip_to, frame_to):
        pl.semaphore_signal(
            barrier, inc=1, device_id=(clip_to, frame_to), device_id_type=MESH
        )

    def greet_line(i):
        greet(lax.rem(clip + i + 1, XH * ZS), frame)

    def greet_frame(i):
        greet(clip, lax.rem(frame + i + 1, FRAMES))

    def greet_plane(i):
        greet((1 - xh) * ZS + z, lax.rem(frame + 2 * (i + 1), FRAMES))

    loop(XH * ZS - 1, greet_line)
    loop(FRAMES - 1, greet_frame)
    loop(CHIPS - 1, greet_plane)

    zero = jnp.zeros((PAD, 3 * C), BF16)
    for buffer in (hcat, mgcat.at[0], mgcat.at[1]):
        buffer[0:PAD, :] = zero
        buffer[PAD + POS : PAD + POS + PAD, :] = zero

    copies[0].wait()
    values = clips_v[...].astype(F32)
    own_sum = group_spread(jnp.sum(values, axis=0, keepdims=True))
    own_mean = own_sum / (POS * (C // GROUPS))
    offset = values - own_mean
    own_squares = group_spread(jnp.sum(offset * offset, axis=0, keepdims=True))
    stat_tx[:, 0:C] = own_sum
    stat_tx[:, C : 2 * C] = own_squares
    copies[1].wait()
    for k in range(3):
        w_time_t[k] = w_time_v[k].T
    copies[2].wait()
    for p in range(3):
        for j in range(3):
            w_space_t[p, j * C : (j + 1) * C, :] = w_space_v[p, j * C : (j + 1) * C, :].T

    pl.semaphore_wait(barrier, XH * ZS - 1 + FRAMES - 1 + CHIPS - 1)

    def share_stats(i):
        remote(
            stat_tx, stat_rx.at[i], send_sem.at[0], recv_sem.at[0],
            clip, lax.rem(frame + i + 1, FRAMES),
        ).start()

    loop(FRAMES - 1, share_stats)

    before = lax.rem(frame + FRAMES - 2, FRAMES)
    after = lax.rem(frame + 2, FRAMES)
    for n in range(CHUNKS):
        rows = pl.ds(n * PIECE, PIECE)
        remote(
            cot.at[rows], cot4.at[2 + core, rows], send_sem.at[1], piece_sem.at[n], clip, before
        ).start()
    remote(cot, cot4.at[core], send_sem.at[2], recv_sem.at[2], clip, sibling).start()

    wait_for(stat_rx, recv_sem.at[0])
    own = stat_tx[...]
    sums = own[:, 0:C]
    squares = own[:, C : 2 * C]
    for i in range(FRAMES - 1):
        sums = sums + stat_rx[i, :, 0:C]
        squares = squares + stat_rx[i, :, C : 2 * C]
    center = sums / members
    part = POS * (C // GROUPS)
    away = own[:, 0:C] / part - center
    spread = away * away
    for i in range(FRAMES - 1):
        away = stat_rx[i, :, 0:C] / part - center
        spread = spread + away * away
    variance = (squares + part * spread) / members
    inv_std = lax.rsqrt(variance + EPSILON)

    column = lax.rem(lax.broadcasted_iota(jnp.int32, (POS, C), 0), COLS)
    normed = (clips_v[...].astype(F32) - center) * inv_std
    act = normed * gain[...] + shift[...]
    act_s[...] = act
    hidden = act / (1.0 + jnp.exp(-act))
    for j in range(3):
        hcat[PAD : PAD + POS, j * C : (j + 1) * C] = shifted(hidden, j - 1, column).astype(BF16)
    even, odd = by_parity(hidden.astype(BF16).T)
    first = core == 0
    h_tx[...] = jnp.where(first, odd, even)
    h_t[core] = jnp.where(first, even, odd)
    remote(h_tx, h_t.at[core], send_sem.at[3], recv_sem.at[3], clip, sibling).start()

    for n in range(CHUNKS):
        rows = pl.ds(n * PIECE, PIECE)
        wait_for(cot4.at[2 + core, rows], piece_sem.at[n])
        remote(
            cot4.at[2 + core, rows], cot4.at[2 + core, rows],
            send_sem.at[4], recv_sem.at[4], clip, sibling,
        ).start()

    mixed = dot(hcat[0:POS, :], w_space_v[0])
    for p in range(1, 3):
        mixed = mixed + dot(hcat[p * COLS : p * COLS + POS, :], w_space_v[p])
    mixed = mixed.astype(BF16)
    mixed_own[...] = mixed
    even, odd = by_parity(mixed.T)
    m_tx[...] = jnp.where(first, odd, even)
    m_t[core] = jnp.where(first, even, odd)
    remote(m_tx, m_t.at[core], send_sem.at[5], recv_sem.at[5], clip, sibling).start()

    copies[3].wait()
    wait_for(cot4.at[0], recv_sem.at[2])
    wait_for(cot4.at[0], recv_sem.at[4])
    wait_for(cot4.at[0], send_sem.at[4])

    @pl.when(q == CHIPS - 1)
    def _():
        cot4[2] = jnp.zeros((POS, C), BF16)
        cot4[3] = jnp.zeros((POS, C), BF16)

    for a in range(2):
        mg = dot(cot4[a], w_time_t[0]) + dot(cot4[a + 1], w_time_t[1])
        mg = mg + dot(cot4[a + 2], w_time_t[2])
        mg = mg.astype(BF16).astype(F32)
        for j in range(3):
            mgcat[a, PAD : PAD + POS, j * C : (j + 1) * C] = shifted(mg, 1 - j, column).astype(BF16)

    wait_for(h_t.at[0], recv_sem.at[3])
    for p in range(3):
        rows = pl.ds((2 - p) * COLS, POS)
        total = dot(h_t[0], mgcat[0, rows, :]) + dot(h_t[1], mgcat[1, rows, :])
        total = total.astype(BF16)
        for half in range(2):
            for to in range(CHIPS):
                for j in range(3):
                    rs_tx_a[half * CHIPS + to, 3 * p + j] = total[
                        to * 16 : to * 16 + 16, j * C + half * 128 : j * C + half * 128 + 128
                    ]

    def plane_target(i):
        r = i + 1
        xh_to = lax.rem(xh + r // CHIPS, XH)
        q_to = lax.rem(q + lax.rem(r, CHIPS), CHIPS)
        return xh_to * CHIPS + q_to, xh_to * ZS + z, 2 * q_to + core

    def scatter_a(i):
        to, clip_to, frame_to = plane_target(i)
        remote(
            rs_tx_a.at[to], rs_rx_a.at[i], send_sem.at[6], recv_sem.at[6], clip_to, frame_to
        ).start()

    loop(XH * CHIPS - 1, scatter_a)

    wait_for(m_t.at[0], recv_sem.at[5])
    for k in range(3):
        total = (dot(m_t[0], cot4[k]) + dot(m_t[1], cot4[k + 1])).astype(BF16)
        for half in range(2):
            for to in range(CHIPS):
                rs_tx_b[half * CHIPS + to, k] = total[
                    to * 16 : to * 16 + 16, half * 128 : half * 128 + 128
                ]

    def scatter_b(i):
        to, clip_to, frame_to = plane_target(i)
        remote(
            rs_tx_b.at[to], rs_rx_b.at[i], send_sem.at[7], recv_sem.at[7], clip_to, frame_to
        ).start()

    loop(XH * CHIPS - 1, scatter_b)

    remote(mixed_own, mixed_halo, send_sem.at[8], recv_sem.at[8], clip, after).start()

    hidden_grad = dot(mgcat[core, 2 * COLS : 2 * COLS + POS, :], w_space_t[0])
    for p in range(1, 3):
        rows = pl.ds((2 - p) * COLS, POS)
        hidden_grad = hidden_grad + dot(mgcat[core, rows, :], w_space_t[p])
    act = act_s[...]
    s = 1.0 / (1.0 + jnp.exp(-act))
    ng = hidden_grad * s * (1.0 + act * (1.0 - s)) * gain[...]
    ng_s[...] = ng
    normed = (clips_v[...].astype(F32) - center) * inv_std
    mean_tx[:, 0:C] = group_spread(jnp.sum(ng, axis=0, keepdims=True))
    mean_tx[:, C : 2 * C] = group_spread(jnp.sum(ng * normed, axis=0, keepdims=True))

    def share_means(i):
        remote(
            mean_tx, mean_rx.at[i], send_sem.at[9], recv_sem.at[9],
            clip, lax.rem(frame + i + 1, FRAMES),
        ).start()

    loop(FRAMES - 1, share_means)

    me = xh * CHIPS + q

    def along_z(k):
        @pl.when(k != z)
        def _():
            remote(
                z_tx.at[k], z_rx.at[lax.rem(z - k + ZS, ZS) - 1],
                send_sem.at[10], recv_sem.at[10], xh * ZS + k, frame,
            ).start()

    wait_for(rs_rx_a, recv_sem.at[6])
    for k in range(9):
        total = rs_tx_a[me, k].astype(F32)
        for i in range(XH * CHIPS - 1):
            total = total + rs_rx_a[i, k].astype(F32)
        z_tx[k] = total
    loop(9, along_z)
    wait_for(rs_rx_b, recv_sem.at[7])
    for k in range(3):
        total = rs_tx_b[me, k].astype(F32)
        for i in range(XH * CHIPS - 1):
            total = total + rs_rx_b[i, k].astype(F32)
        z_tx[9 + k] = total
    loop(3, lambda i: along_z(i + 9))

    wait_for(mean_rx, recv_sem.at[9])
    both = mean_tx[...]
    for i in range(FRAMES - 1):
        both = both + mean_rx[i]
    both = both / members
    m1, m2 = both[:, 0:C], both[:, C : 2 * C]
    normed = (clips_v[...].astype(F32) - center) * inv_std
    grad_out[...] = (
        cot4[core].astype(F32) + inv_std * (ng_s[...] - m1 - normed * m2)
    ).astype(BF16)

    wait_for(mixed_halo, recv_sem.at[8])

    @pl.when(core == 0)
    def _():
        remote(mixed_own, mixed_sib, send_sem.at[11], recv_sem.at[11], clip, sibling).start()

    @pl.when(core == 1)
    def _():
        remote(mixed_halo, mixed_sib, send_sem.at[11], recv_sem.at[11], clip, sibling).start()

    temporal = dot(mixed_own[...], w_time_v[0])
    temporal = temporal + jnp.where(q > 0, dot(mixed_halo[...], w_time_v[2]), 0.0)
    wait_for(mixed_sib, recv_sem.at[11])
    temporal = temporal + jnp.where(frame > 0, dot(mixed_sib[...], w_time_v[1]), 0.0)
    result_out[...] = (clips_v[...].astype(F32) + temporal.astype(BF16).astype(F32)).astype(BF16)

    scale = 1.0 / math.sqrt(XH * ZS * FRAMES * POS)

    @pl.when(z < TAPS)
    def _():
        wait_for(z_rx, recv_sem.at[10])
        total = z_tx[z]
        for i in range(ZS - 1):
            total = total + z_rx[i]
        done = (total * scale).astype(BF16)
        fin_tx[...] = done
        gathered[z * 2 + xh] = done

        def hand_out(i):
            remote(
                fin_tx, gathered.at[z * 2 + xh], send_sem.at[12], recv_sem.at[12],
                lax.rem(clip + i + 1, XH * ZS), frame,
            ).start()

        loop(XH * ZS - 1, hand_out)
        wait_for(gathered.at[pl.ds(0, 2 * TAPS - 1)], recv_sem.at[12])
        wait_for(gathered.at[pl.ds(0, XH * ZS - 1)], send_sem.at[12])
        wait_for(z_tx.at[pl.ds(0, TAPS - 1)], send_sem.at[10])

    @pl.when(z >= TAPS)
    def _():
        wait_for(gathered.at[pl.ds(0, 2 * TAPS)], recv_sem.at[12])
        wait_for(z_tx, send_sem.at[10])

    for k in range(TAPS):
        out = space_out.at[k] if k < 9 else time_out.at[k - 9]
        for half in range(2):
            out[:, half * 128 : half * 128 + 128] = gathered[2 * k + half]

    wait_for(stat_rx, send_sem.at[0])
    wait_for(cot4.at[0], send_sem.at[1])
    wait_for(cot4.at[0], send_sem.at[2])
    wait_for(h_tx, send_sem.at[3])
    wait_for(m_tx, send_sem.at[5])
    wait_for(rs_rx_a, send_sem.at[6])
    wait_for(rs_rx_b, send_sem.at[7])
    wait_for(mixed_own, send_sem.at[8])
    wait_for(mean_rx, send_sem.at[9])
    wait_for(mixed_own, send_sem.at[11])


def per_device(clips, cotangent, norm_gain, norm_shift, w_spatial, w_time):
    anywhere = pl.BlockSpec(memory_space=pl.ANY)
    vmem = pl.BlockSpec(memory_space=pltpu.VMEM)
    result, grad, space, time = pl.pallas_call(
        kernel,
        name="video_block",
        out_shape=(
            jax.ShapeDtypeStruct((POS, C), BF16),
            jax.ShapeDtypeStruct((POS, C), BF16),
            jax.ShapeDtypeStruct((9, 16, C), BF16),
            jax.ShapeDtypeStruct((3, 16, C), BF16),
        ),
        in_specs=[anywhere, anywhere, vmem, vmem, anywhere, anywhere],
        out_specs=(vmem, vmem, vmem, vmem),
        scratch_shapes=[
            pltpu.VMEM((POS, C), BF16),
            pltpu.VMEM((4, POS, C), BF16),
            pltpu.VMEM((3, 3 * C, C), BF16),
            pltpu.VMEM((3, C, C), BF16),
            pltpu.VMEM((3, 3 * C, C), BF16),
            pltpu.VMEM((3, C, C), BF16),
            pltpu.VMEM((POS + 2 * PAD, 3 * C), BF16),
            pltpu.VMEM((2, POS + 2 * PAD, 3 * C), BF16),
            pltpu.VMEM((POS, C), F32),
            pltpu.VMEM((POS, C), F32),
            pltpu.VMEM((2, 128, POS), BF16),
            pltpu.VMEM((128, POS), BF16),
            pltpu.VMEM((2, 128, POS), BF16),
            pltpu.VMEM((128, POS), BF16),
            pltpu.VMEM((POS, C), BF16),
            pltpu.VMEM((POS, C), BF16),
            pltpu.VMEM((POS, C), BF16),
            pltpu.VMEM((1, 2 * C), F32),
            pltpu.VMEM((FRAMES - 1, 1, 2 * C), F32),
            pltpu.VMEM((1, 2 * C), F32),
            pltpu.VMEM((FRAMES - 1, 1, 2 * C), F32),
            pltpu.VMEM((XH * CHIPS, 9, 16, 128), BF16),
            pltpu.VMEM((XH * CHIPS - 1, 9, 16, 128), BF16),
            pltpu.VMEM((XH * CHIPS, 3, 16, 128), BF16),
            pltpu.VMEM((XH * CHIPS - 1, 3, 16, 128), BF16),
            pltpu.VMEM((TAPS, 16, 128), F32),
            pltpu.VMEM((ZS - 1, 16, 128), F32),
            pltpu.VMEM((16, 128), BF16),
            pltpu.VMEM((XH * ZS - 1, 16, 128), BF16),
            pltpu.SemaphoreType.DMA((4,)),
            pltpu.SemaphoreType.DMA((13,)),
            pltpu.SemaphoreType.DMA((13,)),
            pltpu.SemaphoreType.DMA((CHUNKS,)),
        ],
        compiler_params=pltpu.CompilerParams(
            collective_id=0, has_side_effects=True, vmem_limit_bytes=40 * 2**20
        ),
    )(
        clips.reshape(POS, C),
        cotangent.reshape(POS, C),
        norm_gain.reshape(1, C),
        norm_shift.reshape(1, C),
        w_spatial.reshape(3, 3 * C, C),
        w_time,
    )
    return (
        result.reshape(clips.shape),
        grad.reshape(clips.shape),
        space.reshape(3, 3, 16, C),
        time,
    )


def solution(mesh):
    placed = (
        P("clip", "frame", None, None, None),
        P("clip", "frame", None, None, None),
        P(),
        P(),
        P(),
        P(),
    )
    return jax.shard_map(
        per_device,
        mesh=mesh,
        in_specs=placed,
        out_specs=(
            P("clip", "frame", None, None, None),
            P("clip", "frame", None, None, None),
            P(None, None, "frame", None),
            P(None, "frame", None),
        ),
        check_vma=False,
    )
```

time: 529 us -> 69.6 us (0.13)
  the two profiles are of different devices: /device:TPU:16 before, /device:TPU:8 now
where the time goes in v1:
time: 69.6 us; the launch traced here: 69.3 us
  Pallas kernels  60.4 us (87%)
  local copies, waits for them, and re-layouts  8.16 us (12%)
    pallas_call x1, Pallas kernels, per_device(): pl.pallas_call(kernel, name='video_block', out_shape=(jax.ShapeDtypeStruc...  60.4 us
    unnamed x16, local copies, waits for them, and re-layouts  8.16 us

profile of v1, /device:TPU:8, one launch (start us, length us, event | category | flops | bytes accessed | tf_op | source)
XLA Modules:
  0.0 69.3 jit_solution(4987600005937683605)
XLA Ops:
  0.6 0.0 copy-start
  0.6 1.3 %copy-done = bf16[3,3,256,256]{3,2,1,0:T(8,128)(2,1)S(1)} copy-done((bf16[3,3,256,256]{3,2,1,0:T(8,128)(2,1)S(1)}, bf16[3,3,256,256]{3,2,1,0:T(8,128)(2,1)}, u32[]{:S(2)}) %copy-start) | copy-done | bytes 1179672
  1.9 0.0 copy-start.1
  1.9 1.0 %copy-done.1 = bf16[3,256,256]{2,1,0:T(8,128)(2,1)S(1)} copy-done((bf16[3,256,256]{2,1,0:T(8,128)(2,1)S(1)}, bf16[3,256,256]{2,1,0:T(8,128)(2,1)}, u32[]{:S(2)}) %copy-start.1) | copy-done | bytes 393240
  2.9 0.0 copy-start.2
  2.9 0.9 %copy-done.2 = bf16[1,1,16,32,256]{4,3,2,1,0:T(8,128)(2,1)S(1)} copy-done((bf16[1,1,16,32,256]{4,3,2,1,0:T(8,128)(2,1)S(1)}, bf16[1,1,16,32,256]{4,3,2,1,0:T(8,128)(2,1)}, u32[]{:S(2)}) %copy-start.2) | copy-done | bytes 262168
  3.9 0.0 copy-start.3
  3.9 0.9 %copy-done.3 = bf16[1,1,16,32,256]{4,3,2,1,0:T(8,128)(2,1)S(1)} copy-done((bf16[1,1,16,32,256]{4,3,2,1,0:T(8,128)(2,1)S(1)}, bf16[1,1,16,32,256]{4,3,2,1,0:T(8,128)(2,1)}, u32[]{:S(2)}) %copy-start.3) | copy-done | bytes 262168
  4.8 0.0 copy-start.4
  4.8 0.7 copy-done.4
  5.5 0.0 copy-start.5
  5.5 0.7 copy-done.5
  6.2 60.4 %video_block.1 = (bf16[512,256]{1,0:T(8,128)(2,1)S(1)}, bf16[512,256]{1,0:T(8,128)(2,1)S(1)}, bf16[9,16,256]{2,1,0:T(8,128)(2,1)S(1)}, bf16[3,16,256]{2,1,0:T(8,128)(2,1)S(1)}) custom-call(bf16[512,256]{1,0:T(8,128)(2,1)S(1)} %bitcast.9, bf16[512,256]{1,0:T(8,128)(2,1)S(1)} %bitcast.10, f32[1,256]{1,0:T(1,128)S(1)} %bitcast.14, f32[1,256]{1,0:T(1,128)S(1)} %bitcast.15, ...), custom_call_target="tpu_custom_call" | custom-call | tf_op jit(solution)/shard_map/video_block/pallas_call | solution.py:395
  66.6 0.7 %copy.14 = bf16[1,1,16,32,256]{4,3,2,1,0:T(8,128)(2,1)} copy(bf16[1,1,16,32,256]{4,3,2,1,0:T(8,128)(2,1)S(1)} %bitcast.12) | data formatting | bytes 524288
  67.3 0.7 %copy.15 = bf16[1,1,16,32,256]{4,3,2,1,0:T(8,128)(2,1)} copy(bf16[1,1,16,32,256]{4,3,2,1,0:T(8,128)(2,1)S(1)} %bitcast.11) | data formatting | bytes 524288
  68.0 0.6 copy.16
  68.7 0.6 copy.17
Async XLA Ops:
  0.6 1.3 %copy-start = (bf16[3,3,256,256]{3,2,1,0:T(8,128)(2,1)S(1)}, bf16[3,3,256,256]{3,2,1,0:T(8,128)(2,1)}, u32[]{:S(2)}) copy-start(bf16[3,3,256,256]{3,2,1,0:T(8,128)(2,1)} %param.10) | copy-start | bytes 3538948
  1.9 1.0 %copy-start.1 = (bf16[3,256,256]{2,1,0:T(8,128)(2,1)S(1)}, bf16[3,256,256]{2,1,0:T(8,128)(2,1)}, u32[]{:S(2)}) copy-start(bf16[3,256,256]{2,1,0:T(8,128)(2,1)} %w_time.1) | copy-start | bytes 1179652
  2.9 0.9 %copy-start.2 = (bf16[1,1,16,32,256]{4,3,2,1,0:T(8,128)(2,1)S(1)}, bf16[1,1,16,32,256]{4,3,2,1,0:T(8,128)(2,1)}, u32[]{:S(2)}) copy-start(bf16[1,1,16,32,256]{4,3,2,1,0:T(8,128)(2,1)} %param.6) | copy-start | bytes 786436
  3.9 0.9 %copy-start.3 = (bf16[1,1,16,32,256]{4,3,2,1,0:T(8,128)(2,1)S(1)}, bf16[1,1,16,32,256]{4,3,2,1,0:T(8,128)(2,1)}, u32[]{:S(2)}) copy-start(bf16[1,1,16,32,256]{4,3,2,1,0:T(8,128)(2,1)} %param.7) | copy-start | bytes 786436
  4.8 0.7 copy-start.4
  5.5 0.7 copy-start.5

commit v2 on v1

--- a/solution.py
+++ b/solution.py
@@ -18,6 +18,12 @@
 POS = ROWS * COLS
 PAD = COLS
 TAPS = 12
+VMEM_BYTES = 60 * 2**20
+
+PLANE_ORDER = (
+    (2, 2), (1, 0), (0, 1), (2, 1), (0, 3), (3, 0), (1, 2), (1, 1),
+    (2, 3), (3, 3), (3, 2), (0, 2), (2, 0), (3, 1), (1, 3),
+)
 CHUNKS = 4
 PIECE = POS // CHUNKS
 
@@ -52,6 +58,10 @@
     lax.fori_loop(0, count, step, 0)
 
 
+def far_first(i):
+    return ZS // 2 + ((i + 1) // 2) * (1 - 2 * lax.rem(i, 2))
+
+
 def group_spread(row):
     lane = lax.broadcasted_iota(jnp.int32, row.shape, 1)
     for bit in (1, 2, 4):
@@ -78,13 +88,13 @@
 
 
 def kernel(
-    clips, cot, gain, shift, w_space, w_time,
-    result_out, grad_out, space_out, time_out,
+    clips, cot, gain_in, shift_in, w_space, w_time,
+    result_out, grad_out, taps_out,
     clips_v, cot4, w_space_v, w_time_v, w_space_t, w_time_t,
     hcat, mgcat, act_s, ng_s, h_t, h_tx, m_t, m_tx, mixed_own, mixed_halo, mixed_sib,
     stat_tx, stat_rx, mean_tx, mean_rx,
     rs_tx_a, rs_rx_a, rs_tx_b, rs_rx_b, z_tx, z_rx, fin_tx, gathered,
-    local_sem, send_sem, recv_sem, piece_sem,
+    gain, shift, result_v, grad_v, taps_v, local_sem, send_sem, recv_sem, piece_sem, known,
 ):
     clip = lax.axis_index("clip")
     frame = lax.axis_index("frame")
@@ -98,6 +108,8 @@
         pltpu.make_async_copy(w_time, w_time_v, local_sem.at[1]),
         pltpu.make_async_copy(w_space, w_space_v, local_sem.at[2]),
         pltpu.make_async_copy(cot, cot4.at[core], local_sem.at[3]),
+        pltpu.make_async_copy(gain_in, gain, local_sem.at[4]),
+        pltpu.make_async_copy(shift_in, shift, local_sem.at[5]),
     ]
     for copy in copies:
         copy.start()
@@ -109,18 +121,25 @@
             barrier, inc=1, device_id=(clip_to, frame_to), device_id_type=MESH
         )
 
-    def greet_line(i):
-        greet(lax.rem(clip + i + 1, XH * ZS), frame)
-
     def greet_frame(i):
         greet(clip, lax.rem(frame + i + 1, FRAMES))
 
     def greet_plane(i):
-        greet((1 - xh) * ZS + z, lax.rem(frame + 2 * (i + 1), FRAMES))
-
-    loop(XH * ZS - 1, greet_line)
+        greet((1 - xh) * ZS + z, lax.rem(frame + 2 * i, FRAMES))
+
+    def along(by):
+        return xh * ZS + lax.rem(z + by + ZS, ZS)
+
+    def tell(step):
+        for by in (-(2**step), 2**step):
+            pl.semaphore_signal(
+                known.at[step], inc=1, device_id=(along(by), frame), device_id_type=MESH
+            )
+
+    loop(CHIPS, greet_plane)
+    greet(along(-1), frame)
+    greet(along(1), frame)
     loop(FRAMES - 1, greet_frame)
-    loop(CHIPS - 1, greet_plane)
 
     zero = jnp.zeros((PAD, 3 * C), BF16)
     for buffer in (hcat, mgcat.at[0], mgcat.at[1]):
@@ -138,12 +157,14 @@
     copies[1].wait()
     for k in range(3):
         w_time_t[k] = w_time_v[k].T
+    copies[4].wait()
+    copies[5].wait()
     copies[2].wait()
     for p in range(3):
         for j in range(3):
             w_space_t[p, j * C : (j + 1) * C, :] = w_space_v[p, j * C : (j + 1) * C, :].T
 
-    pl.semaphore_wait(barrier, XH * ZS - 1 + FRAMES - 1 + CHIPS - 1)
+    pl.semaphore_wait(barrier, CHIPS + 2 + FRAMES - 1)
 
     def share_stats(i):
         remote(
@@ -161,6 +182,8 @@
             cot.at[rows], cot4.at[2 + core, rows], send_sem.at[1], piece_sem.at[n], clip, before
         ).start()
     remote(cot, cot4.at[core], send_sem.at[2], recv_sem.at[2], clip, sibling).start()
+
+    tell(0)
 
     wait_for(stat_rx, recv_sem.at[0])
     own = stat_tx[...]
@@ -192,6 +215,9 @@
     h_t[core] = jnp.where(first, even, odd)
     remote(h_tx, h_t.at[core], send_sem.at[3], recv_sem.at[3], clip, sibling).start()
 
+    pl.semaphore_wait(known.at[0], 2)
+    tell(1)
+
     for n in range(CHUNKS):
         rows = pl.ds(n * PIECE, PIECE)
         wait_for(cot4.at[2 + core, rows], piece_sem.at[n])
@@ -209,6 +235,9 @@
     m_tx[...] = jnp.where(first, odd, even)
     m_t[core] = jnp.where(first, even, odd)
     remote(m_tx, m_t.at[core], send_sem.at[5], recv_sem.at[5], clip, sibling).start()
+
+    pl.semaphore_wait(known.at[1], 2)
+    tell(2)
 
     copies[3].wait()
     wait_for(cot4.at[0], recv_sem.at[2])
@@ -239,19 +268,17 @@
                         to * 16 : to * 16 + 16, j * C + half * 128 : j * C + half * 128 + 128
                     ]
 
-    def plane_target(i):
-        r = i + 1
-        xh_to = lax.rem(xh + r // CHIPS, XH)
-        q_to = lax.rem(q + lax.rem(r, CHIPS), CHIPS)
-        return xh_to * CHIPS + q_to, xh_to * ZS + z, 2 * q_to + core
-
-    def scatter_a(i):
-        to, clip_to, frame_to = plane_target(i)
-        remote(
-            rs_tx_a.at[to], rs_rx_a.at[i], send_sem.at[6], recv_sem.at[6], clip_to, frame_to
-        ).start()
-
-    loop(XH * CHIPS - 1, scatter_a)
+    def scatter(tx, rx, n):
+        for i, (by_x, by_y) in enumerate(PLANE_ORDER):
+            x = lax.rem(2 * xh + lax.rem(q, 2) + by_x, 2 * XH)
+            y = lax.rem(q // 2 + by_y, CHIPS // 2)
+            xh_to, q_to = x // 2, 2 * y + lax.rem(x, 2)
+            remote(
+                tx.at[xh_to * CHIPS + q_to], rx.at[i], send_sem.at[n], recv_sem.at[n],
+                xh_to * ZS + z, 2 * q_to + core,
+            ).start()
+
+    scatter(rs_tx_a, rs_rx_a, 6)
 
     wait_for(m_t.at[0], recv_sem.at[5])
     for k in range(3):
@@ -262,15 +289,7 @@
                     to * 16 : to * 16 + 16, half * 128 : half * 128 + 128
                 ]
 
-    def scatter_b(i):
-        to, clip_to, frame_to = plane_target(i)
-        remote(
-            rs_tx_b.at[to], rs_rx_b.at[i], send_sem.at[7], recv_sem.at[7], clip_to, frame_to
-        ).start()
-
-    loop(XH * CHIPS - 1, scatter_b)
-
-    remote(mixed_own, mixed_halo, send_sem.at[8], recv_sem.at[8], clip, after).start()
+    scatter(rs_tx_b, rs_rx_b, 7)
 
     hidden_grad = dot(mgcat[core, 2 * COLS : 2 * COLS + POS, :], w_space_t[0])
     for p in range(1, 3):
@@ -294,13 +313,18 @@
 
     me = xh * CHIPS + q
 
-    def along_z(k):
-        @pl.when(k != z)
-        def _():
-            remote(
-                z_tx.at[k], z_rx.at[lax.rem(z - k + ZS, ZS) - 1],
-                send_sem.at[10], recv_sem.at[10], xh * ZS + k, frame,
-            ).start()
+    def along_z(lowest, highest):
+        def send(i):
+            to = lax.rem(z + far_first(i), ZS)
+
+            @pl.when((to >= lowest) & (to < highest))
+            def _():
+                remote(
+                    z_tx.at[to], z_rx.at[ZS - 1 - far_first(i)],
+                    send_sem.at[10], recv_sem.at[10], xh * ZS + to, frame,
+                ).start()
+
+        loop(ZS - 1, send)
 
     wait_for(rs_rx_a, recv_sem.at[6])
     for k in range(9):
@@ -308,14 +332,17 @@
         for i in range(XH * CHIPS - 1):
             total = total + rs_rx_a[i, k].astype(F32)
         z_tx[k] = total
-    loop(9, along_z)
+    pl.semaphore_wait(known.at[2], 2)
+    along_z(0, 9)
     wait_for(rs_rx_b, recv_sem.at[7])
     for k in range(3):
         total = rs_tx_b[me, k].astype(F32)
         for i in range(XH * CHIPS - 1):
             total = total + rs_rx_b[i, k].astype(F32)
         z_tx[9 + k] = total
-    loop(3, lambda i: along_z(i + 9))
+    along_z(9, TAPS)
+
+    remote(mixed_own, mixed_halo, send_sem.at[8], recv_sem.at[8], clip, after).start()
 
     wait_for(mean_rx, recv_sem.at[9])
     both = mean_tx[...]
@@ -324,9 +351,11 @@
     both = both / members
     m1, m2 = both[:, 0:C], both[:, C : 2 * C]
     normed = (clips_v[...].astype(F32) - center) * inv_std
-    grad_out[...] = (
+    grad_v[...] = (
         cot4[core].astype(F32) + inv_std * (ng_s[...] - m1 - normed * m2)
     ).astype(BF16)
+    grad_copy = pltpu.make_async_copy(grad_v, grad_out, local_sem.at[6])
+    grad_copy.start()
 
     wait_for(mixed_halo, recv_sem.at[8])
 
@@ -342,7 +371,9 @@
     temporal = temporal + jnp.where(q > 0, dot(mixed_halo[...], w_time_v[2]), 0.0)
     wait_for(mixed_sib, recv_sem.at[11])
     temporal = temporal + jnp.where(frame > 0, dot(mixed_sib[...], w_time_v[1]), 0.0)
-    result_out[...] = (clips_v[...].astype(F32) + temporal.astype(BF16).astype(F32)).astype(BF16)
+    result_v[...] = (clips_v[...].astype(F32) + temporal.astype(BF16).astype(F32)).astype(BF16)
+    result_copy = pltpu.make_async_copy(result_v, result_out, local_sem.at[7])
+    result_copy.start()
 
     scale = 1.0 / math.sqrt(XH * ZS * FRAMES * POS)
 
@@ -356,13 +387,18 @@
         fin_tx[...] = done
         gathered[z * 2 + xh] = done
 
+        def hand(clip_to):
+            remote(
+                fin_tx, gathered.at[z * 2 + xh], send_sem.at[12], recv_sem.at[12], clip_to, frame
+            ).start()
+
         def hand_out(i):
-            remote(
-                fin_tx, gathered.at[z * 2 + xh], send_sem.at[12], recv_sem.at[12],
-                lax.rem(clip + i + 1, XH * ZS), frame,
-            ).start()
-
-        loop(XH * ZS - 1, hand_out)
+            to = lax.rem(z + far_first(i), ZS)
+            hand((1 - xh) * ZS + to)
+            hand(xh * ZS + to)
+
+        loop(ZS - 1, hand_out)
+        hand((1 - xh) * ZS + z)
         wait_for(gathered.at[pl.ds(0, 2 * TAPS - 1)], recv_sem.at[12])
         wait_for(gathered.at[pl.ds(0, XH * ZS - 1)], send_sem.at[12])
         wait_for(z_tx.at[pl.ds(0, TAPS - 1)], send_sem.at[10])
@@ -373,9 +409,10 @@
         wait_for(z_tx, send_sem.at[10])
 
     for k in range(TAPS):
-        out = space_out.at[k] if k < 9 else time_out.at[k - 9]
         for half in range(2):
-            out[:, half * 128 : half * 128 + 128] = gathered[2 * k + half]
+            taps_v[k, :, half * 128 : half * 128 + 128] = gathered[2 * k + half]
+    taps_copy = pltpu.make_async_copy(taps_v, taps_out, local_sem.at[8])
+    taps_copy.start()
 
     wait_for(stat_rx, send_sem.at[0])
     wait_for(cot4.at[0], send_sem.at[1])
@@ -387,22 +424,48 @@
     wait_for(mixed_own, send_sem.at[8])
     wait_for(mean_rx, send_sem.at[9])
     wait_for(mixed_own, send_sem.at[11])
+    for copy in (grad_copy, result_copy, taps_copy):
+        copy.wait()
+
+
+def write_out(result, grad, taps, result_out, grad_out, space_out, time_out, *scratch):
+    result_v, grad_v, taps_v, in_sem, out_sem = scratch
+    moves = [(taps, taps_v, ((0, 9, space_out), (9, 3, time_out)))]
+    half = POS // 2
+    for source, held, target in ((result, result_v, result_out), (grad, grad_v, grad_out)):
+        for n in range(2):
+            rows = pl.ds(n * half, half)
+            moves.append((source.at[rows], held.at[rows], ((0, half, target.at[rows]),)))
+    into = [
+        pltpu.make_async_copy(source, held, in_sem.at[n])
+        for n, (source, held, _) in enumerate(moves)
+    ]
+    for copy in into:
+        copy.start()
+    back = []
+    for copy, (_, held, parts) in zip(into, moves):
+        copy.wait()
+        for first, count, target in parts:
+            back.append(
+                pltpu.make_async_copy(held.at[pl.ds(first, count)], target, out_sem.at[len(back)])
+            )
+            back[-1].start()
+    for copy in back:
+        copy.wait()
 
 
 def per_device(clips, cotangent, norm_gain, norm_shift, w_spatial, w_time):
-    anywhere = pl.BlockSpec(memory_space=pl.ANY)
-    vmem = pl.BlockSpec(memory_space=pltpu.VMEM)
-    result, grad, space, time = pl.pallas_call(
+    hbm = pl.BlockSpec(memory_space=pltpu.HBM)
+    blocks = pl.pallas_call(
         kernel,
         name="video_block",
         out_shape=(
             jax.ShapeDtypeStruct((POS, C), BF16),
             jax.ShapeDtypeStruct((POS, C), BF16),
-            jax.ShapeDtypeStruct((9, 16, C), BF16),
-            jax.ShapeDtypeStruct((3, 16, C), BF16),
+            jax.ShapeDtypeStruct((TAPS, 16, C), BF16),
         ),
-        in_specs=[anywhere, anywhere, vmem, vmem, anywhere, anywhere],
-        out_specs=(vmem, vmem, vmem, vmem),
+        in_specs=[hbm] * 6,
+        out_specs=(hbm, hbm, hbm),
         scratch_shapes=[
             pltpu.VMEM((POS, C), BF16),
             pltpu.VMEM((4, POS, C), BF16),
@@ -433,13 +496,19 @@
             pltpu.VMEM((ZS - 1, 16, 128), F32),
             pltpu.VMEM((16, 128), BF16),
             pltpu.VMEM((XH * ZS - 1, 16, 128), BF16),
-            pltpu.SemaphoreType.DMA((4,)),
+            pltpu.VMEM((1, C), F32),
+            pltpu.VMEM((1, C), F32),
+            pltpu.VMEM((POS, C), BF16),
+            pltpu.VMEM((POS, C), BF16),
+            pltpu.VMEM((TAPS, 16, C), BF16),
+            pltpu.SemaphoreType.DMA((9,)),
             pltpu.SemaphoreType.DMA((13,)),
             pltpu.SemaphoreType.DMA((13,)),
             pltpu.SemaphoreType.DMA((CHUNKS,)),
+            pltpu.SemaphoreType.REGULAR((3,)),
         ],
         compiler_params=pltpu.CompilerParams(
-            collective_id=0, has_side_effects=True, vmem_limit_bytes=40 * 2**20
+            collective_id=0, has_side_effects=True, vmem_limit_bytes=VMEM_BYTES
         ),
     )(
         clips.reshape(POS, C),
@@ -449,6 +518,26 @@
         w_spatial.reshape(3, 3 * C, C),
         w_time,
     )
+    result, grad, space, time = pl.pallas_call(
+        write_out,
+        name="write_out",
+        out_shape=(
+            jax.ShapeDtypeStruct((POS, C), BF16),
+            jax.ShapeDtypeStruct((POS, C), BF16),
+            jax.ShapeDtypeStruct((9, 16, C), BF16),
+            jax.ShapeDtypeStruct((3, 16, C), BF16),
+        ),
+        in_specs=[hbm, hbm, hbm],
+        out_specs=(hbm, hbm, hbm, hbm),
+        scratch_shapes=[
+            pltpu.VMEM((POS, C), BF16),
+            pltpu.VMEM((POS, C), BF16),
+            pltpu.VMEM((TAPS, 16, C), BF16),
+            pltpu.SemaphoreType.DMA((5,)),
+            pltpu.SemaphoreType.DMA((6,)),
+        ],
+        compiler_params=pltpu.CompilerParams(vmem_limit_bytes=VMEM_BYTES),
+    )(*blocks)
     return (
         result.reshape(clips.shape),
         grad.reshape(clips.shape),

time: 69.6 us -> 61.9 us (0.89)
  the two profiles are of different devices: /device:TPU:8 before, /device:TPU:1 now
where the time goes in v2:
time: 61.9 us; the launch traced here: 61.7 us
  Pallas kernels  61.1 us (99%)
  between operations  0.64 us (1%)
    pallas_call x1, Pallas kernels, per_device(): pl.pallas_call(kernel, name='video_block', out_shape=(jax.ShapeDtypeStruc...  59.2 us
    pallas_call x1, Pallas kernels, per_device(): pl.pallas_call(write_out, name='write_out', out_shape=(jax.ShapeDtypeStru...  1.89 us

profile of v2, /device:TPU:1, one launch (start us, length us, event | category | flops | bytes accessed | tf_op | source)
XLA Modules:
  0.0 61.7 jit_solution(6328985884344788299)
XLA Ops:
  0.6 59.2 %video_block.1 = (bf16[512,256]{1,0:T(8,128)(2,1)}, bf16[512,256]{1,0:T(8,128)(2,1)}, bf16[12,16,256]{2,1,0:T(8,128)(2,1)}) custom-call(bf16[512,256]{1,0:T(8,128)(2,1)} %bitcast.9, bf16[512,256]{1,0:T(8,128)(2,1)} %bitcast.10, f32[1,256]{1,0:T(1,128)} %bitcast.11, f32[1,256]{1,0:T(1,128)} %bitcast.12, bf16[3,768,256]{2,1,0:T(8,128)(2,1)} %bitcast.8, ...), custom_call_target="tpu_custom_call" | custom-call | tf_op jit(solution)/shard_map/video_block/pallas_call | solution.py:459
  59.8 1.9 %write_out.1 = (bf16[512,256]{1,0:T(8,128)(2,1)}, bf16[512,256]{1,0:T(8,128)(2,1)}, bf16[9,16,256]{2,1,0:T(8,128)(2,1)}, bf16[3,16,256]{2,1,0:T(8,128)(2,1)}) custom-call(bf16[512,256]{1,0:T(8,128)(2,1)} %get-tuple-element.11.result, bf16[512,256]{1,0:T(8,128)(2,1)} %get-tuple-element.12.grad, bf16[12,16,256]{2,1,0:T(8,128)(2,1)} %get-tuple-element.13.taps), custom_call_target="tpu_custom_call" | custom-call | tf_op jit(solution)/shard_map/write_out/pallas_call | solution.py:521

commit v3 on v2

--- a/solution.py
+++ b/solution.py
@@ -19,6 +19,11 @@
 PAD = COLS
 TAPS = 12
 VMEM_BYTES = 60 * 2**20
+
+FRAME_ORDER = (
+    (2, 1, 0), (2, 1, 1), (2, 0, 0), (2, 0, 1), (1, 1, 0), (1, 1, 1), (3, 1, 0), (3, 1, 1),
+    (1, 0, 0), (1, 0, 1), (3, 0, 0), (3, 0, 1), (0, 1, 0), (0, 1, 1), (0, 0, 1),
+)
 
 PLANE_ORDER = (
     (2, 2), (1, 0), (0, 1), (2, 1), (0, 3), (3, 0), (1, 2), (1, 1),
@@ -91,7 +96,7 @@
     clips, cot, gain_in, shift_in, w_space, w_time,
     result_out, grad_out, taps_out,
     clips_v, cot4, w_space_v, w_time_v, w_space_t, w_time_t,
-    hcat, mgcat, act_s, ng_s, h_t, h_tx, m_t, m_tx, mixed_own, mixed_halo, mixed_sib,
+    hcat, mgcat, act_s, hid_s, hid_grad_s, ng_s, h_t, h_tx, m_t, m_tx, mixed_own, mixed_halo, mixed_sib,
     stat_tx, stat_rx, mean_tx, mean_rx,
     rs_tx_a, rs_rx_a, rs_tx_b, rs_rx_b, z_tx, z_rx, fin_tx, gathered,
     gain, shift, result_v, grad_v, taps_v, local_sem, send_sem, recv_sem, piece_sem, known,
@@ -103,6 +108,36 @@
     sibling = frame + 1 - 2 * core
     members = FRAMES * POS * (C // GROUPS)
 
+    barrier = pltpu.get_barrier_semaphore()
+
+    def greet(clip_to, frame_to):
+        pl.semaphore_signal(
+            barrier, inc=1, device_id=(clip_to, frame_to), device_id_type=MESH
+        )
+
+    def along(by):
+        return xh * ZS + lax.rem(z + by + ZS, ZS)
+
+    def tell(step):
+        for by in (-(2**step), 2**step):
+            pl.semaphore_signal(
+                known.at[step], inc=1, device_id=(along(by), frame), device_id_type=MESH
+            )
+
+    y, x_lo = q // 2, lax.rem(q, 2)
+    other = (1 - xh) * ZS + z
+    mates = [
+        4 * lax.rem(y + by_y, CHIPS // 2)
+        + 2 * (1 - x_lo if by_x else x_lo)
+        + (1 - core if by_core else core)
+        for by_y, by_x, by_core in FRAME_ORDER
+    ]
+    for mate in mates:
+        greet(clip, mate)
+    greet(other, frame)
+    greet(along(-1), frame)
+    greet(along(1), frame)
+
     copies = [
         pltpu.make_async_copy(clips, clips_v, local_sem.at[0]),
         pltpu.make_async_copy(w_time, w_time_v, local_sem.at[1]),
@@ -114,33 +149,6 @@
     for copy in copies:
         copy.start()
 
-    barrier = pltpu.get_barrier_semaphore()
-
-    def greet(clip_to, frame_to):
-        pl.semaphore_signal(
-            barrier, inc=1, device_id=(clip_to, frame_to), device_id_type=MESH
-        )
-
-    def greet_frame(i):
-        greet(clip, lax.rem(frame + i + 1, FRAMES))
-
-    def greet_plane(i):
-        greet((1 - xh) * ZS + z, lax.rem(frame + 2 * i, FRAMES))
-
-    def along(by):
-        return xh * ZS + lax.rem(z + by + ZS, ZS)
-
-    def tell(step):
-        for by in (-(2**step), 2**step):
-            pl.semaphore_signal(
-                known.at[step], inc=1, device_id=(along(by), frame), device_id_type=MESH
-            )
-
-    loop(CHIPS, greet_plane)
-    greet(along(-1), frame)
-    greet(along(1), frame)
-    loop(FRAMES - 1, greet_frame)
-
     zero = jnp.zeros((PAD, 3 * C), BF16)
     for buffer in (hcat, mgcat.at[0], mgcat.at[1]):
         buffer[0:PAD, :] = zero
@@ -154,6 +162,23 @@
     own_squares = group_spread(jnp.sum(offset * offset, axis=0, keepdims=True))
     stat_tx[:, 0:C] = own_sum
     stat_tx[:, C : 2 * C] = own_squares
+    pl.semaphore_wait(barrier, FRAMES - 1 + 3)
+
+    for i, mate in enumerate(mates):
+        remote(stat_tx, stat_rx.at[i], send_sem.at[0], recv_sem.at[0], clip, mate).start()
+
+    before = lax.rem(frame + FRAMES - 2, FRAMES)
+    after = lax.rem(frame + 2, FRAMES)
+    for n in range(CHUNKS):
+        rows = pl.ds(n * PIECE, PIECE)
+        remote(
+            cot.at[rows], cot4.at[2 + core, rows], send_sem.at[1], piece_sem.at[n], clip, before
+        ).start()
+    remote(cot, cot4.at[core], send_sem.at[2], recv_sem.at[2], clip, sibling).start()
+
+    tell(0)
+    pl.semaphore_signal(known.at[3], inc=1, device_id=(other, frame), device_id_type=MESH)
+
     copies[1].wait()
     for k in range(3):
         w_time_t[k] = w_time_v[k].T
@@ -163,27 +188,6 @@
     for p in range(3):
         for j in range(3):
             w_space_t[p, j * C : (j + 1) * C, :] = w_space_v[p, j * C : (j + 1) * C, :].T
-
-    pl.semaphore_wait(barrier, CHIPS + 2 + FRAMES - 1)
-
-    def share_stats(i):
-        remote(
-            stat_tx, stat_rx.at[i], send_sem.at[0], recv_sem.at[0],
-            clip, lax.rem(frame + i + 1, FRAMES),
-        ).start()
-
-    loop(FRAMES - 1, share_stats)
-
-    before = lax.rem(frame + FRAMES - 2, FRAMES)
-    after = lax.rem(frame + 2, FRAMES)
-    for n in range(CHUNKS):
-        rows = pl.ds(n * PIECE, PIECE)
-        remote(
-            cot.at[rows], cot4.at[2 + core, rows], send_sem.at[1], piece_sem.at[n], clip, before
-        ).start()
-    remote(cot, cot4.at[core], send_sem.at[2], recv_sem.at[2], clip, sibling).start()
-
-    tell(0)
 
     wait_for(stat_rx, recv_sem.at[0])
     own = stat_tx[...]
@@ -207,16 +211,12 @@
     act = normed * gain[...] + shift[...]
     act_s[...] = act
     hidden = act / (1.0 + jnp.exp(-act))
-    for j in range(3):
-        hcat[PAD : PAD + POS, j * C : (j + 1) * C] = shifted(hidden, j - 1, column).astype(BF16)
+    hid_s[...] = hidden
     even, odd = by_parity(hidden.astype(BF16).T)
     first = core == 0
     h_tx[...] = jnp.where(first, odd, even)
     h_t[core] = jnp.where(first, even, odd)
     remote(h_tx, h_t.at[core], send_sem.at[3], recv_sem.at[3], clip, sibling).start()
-
-    pl.semaphore_wait(known.at[0], 2)
-    tell(1)
 
     for n in range(CHUNKS):
         rows = pl.ds(n * PIECE, PIECE)
@@ -226,21 +226,10 @@
             send_sem.at[4], recv_sem.at[4], clip, sibling,
         ).start()
 
-    mixed = dot(hcat[0:POS, :], w_space_v[0])
-    for p in range(1, 3):
-        mixed = mixed + dot(hcat[p * COLS : p * COLS + POS, :], w_space_v[p])
-    mixed = mixed.astype(BF16)
-    mixed_own[...] = mixed
-    even, odd = by_parity(mixed.T)
-    m_tx[...] = jnp.where(first, odd, even)
-    m_t[core] = jnp.where(first, even, odd)
-    remote(m_tx, m_t.at[core], send_sem.at[5], recv_sem.at[5], clip, sibling).start()
-
-    pl.semaphore_wait(known.at[1], 2)
-    tell(2)
-
     copies[3].wait()
     wait_for(cot4.at[0], recv_sem.at[2])
+    ng_s[...] = dot(cot4[0], w_time_t[0]) + dot(cot4[1], w_time_t[1])
+    hid_grad_s[...] = dot(cot4[1], w_time_t[0])
     wait_for(cot4.at[0], recv_sem.at[4])
     wait_for(cot4.at[0], send_sem.at[4])
 
@@ -250,11 +239,16 @@
         cot4[3] = jnp.zeros((POS, C), BF16)
 
     for a in range(2):
-        mg = dot(cot4[a], w_time_t[0]) + dot(cot4[a + 1], w_time_t[1])
-        mg = mg + dot(cot4[a + 2], w_time_t[2])
+        if a == 0:
+            mg = ng_s[...] + dot(cot4[2], w_time_t[2])
+        else:
+            mg = hid_grad_s[...] + dot(cot4[2], w_time_t[1]) + dot(cot4[3], w_time_t[2])
         mg = mg.astype(BF16).astype(F32)
         for j in range(3):
             mgcat[a, PAD : PAD + POS, j * C : (j + 1) * C] = shifted(mg, 1 - j, column).astype(BF16)
+
+    pl.semaphore_wait(known.at[0], 2)
+    tell(1)
 
     wait_for(h_t.at[0], recv_sem.at[3])
     for p in range(3):
@@ -278,7 +272,21 @@
                 xh_to * ZS + z, 2 * q_to + core,
             ).start()
 
+    pl.semaphore_wait(known.at[3], 1)
     scatter(rs_tx_a, rs_rx_a, 6)
+
+    hidden = hid_s[...]
+    for j in range(3):
+        hcat[PAD : PAD + POS, j * C : (j + 1) * C] = shifted(hidden, j - 1, column).astype(BF16)
+    mixed = dot(hcat[0:POS, :], w_space_v[0])
+    for p in range(1, 3):
+        mixed = mixed + dot(hcat[p * COLS : p * COLS + POS, :], w_space_v[p])
+    mixed = mixed.astype(BF16)
+    mixed_own[...] = mixed
+    even, odd = by_parity(mixed.T)
+    m_tx[...] = jnp.where(first, odd, even)
+    m_t[core] = jnp.where(first, even, odd)
+    remote(m_tx, m_t.at[core], send_sem.at[5], recv_sem.at[5], clip, sibling).start()
 
     wait_for(m_t.at[0], recv_sem.at[5])
     for k in range(3):
@@ -290,6 +298,8 @@
                 ]
 
     scatter(rs_tx_b, rs_rx_b, 7)
+    pl.semaphore_wait(known.at[1], 2)
+    tell(2)
 
     hidden_grad = dot(mgcat[core, 2 * COLS : 2 * COLS + POS, :], w_space_t[0])
     for p in range(1, 3):
@@ -303,13 +313,8 @@
     mean_tx[:, 0:C] = group_spread(jnp.sum(ng, axis=0, keepdims=True))
     mean_tx[:, C : 2 * C] = group_spread(jnp.sum(ng * normed, axis=0, keepdims=True))
 
-    def share_means(i):
-        remote(
-            mean_tx, mean_rx.at[i], send_sem.at[9], recv_sem.at[9],
-            clip, lax.rem(frame + i + 1, FRAMES),
-        ).start()
-
-    loop(FRAMES - 1, share_means)
+    for i, mate in enumerate(mates):
+        remote(mean_tx, mean_rx.at[i], send_sem.at[9], recv_sem.at[9], clip, mate).start()
 
     me = xh * CHIPS + q
 
@@ -317,10 +322,12 @@
         def send(i):
             to = lax.rem(z + far_first(i), ZS)
 
-            @pl.when((to >= lowest) & (to < highest))
+            tap = to - to // 4
+
+            @pl.when((lax.rem(to, 4) < 3) & (tap >= lowest) & (tap < highest))
             def _():
                 remote(
-                    z_tx.at[to], z_rx.at[ZS - 1 - far_first(i)],
+                    z_tx.at[tap], z_rx.at[ZS - 1 - far_first(i)],
                     send_sem.at[10], recv_sem.at[10], xh * ZS + to, frame,
                 ).start()
 
@@ -357,6 +364,32 @@
     grad_copy = pltpu.make_async_copy(grad_v, grad_out, local_sem.at[6])
     grad_copy.start()
 
+    scale = 1.0 / math.sqrt(XH * ZS * FRAMES * POS)
+
+    @pl.when(lax.rem(z, 4) < 3)
+    def _():
+        wait_for(z_rx, recv_sem.at[10])
+        tap = z - z // 4
+        total = z_tx[tap]
+        for i in range(ZS - 1):
+            total = total + z_rx[i]
+        done = (total * scale).astype(BF16)
+        fin_tx[...] = done
+        gathered[tap * 2 + xh] = done
+
+        def hand(clip_to):
+            remote(
+                fin_tx, gathered.at[tap * 2 + xh], send_sem.at[12], recv_sem.at[12], clip_to, frame
+            ).start()
+
+        def hand_out(i):
+            to = lax.rem(z + far_first(i), ZS)
+            hand((1 - xh) * ZS + to)
+            hand(xh * ZS + to)
+
+        loop(ZS - 1, hand_out)
+        hand((1 - xh) * ZS + z)
+
     wait_for(mixed_halo, recv_sem.at[8])
 
     @pl.when(core == 0)
@@ -375,35 +408,13 @@
     result_copy = pltpu.make_async_copy(result_v, result_out, local_sem.at[7])
     result_copy.start()
 
-    scale = 1.0 / math.sqrt(XH * ZS * FRAMES * POS)
-
-    @pl.when(z < TAPS)
+    @pl.when(lax.rem(z, 4) < 3)
     def _():
-        wait_for(z_rx, recv_sem.at[10])
-        total = z_tx[z]
-        for i in range(ZS - 1):
-            total = total + z_rx[i]
-        done = (total * scale).astype(BF16)
-        fin_tx[...] = done
-        gathered[z * 2 + xh] = done
-
-        def hand(clip_to):
-            remote(
-                fin_tx, gathered.at[z * 2 + xh], send_sem.at[12], recv_sem.at[12], clip_to, frame
-            ).start()
-
-        def hand_out(i):
-            to = lax.rem(z + far_first(i), ZS)
-            hand((1 - xh) * ZS + to)
-            hand(xh * ZS + to)
-
-        loop(ZS - 1, hand_out)
-        hand((1 - xh) * ZS + z)
         wait_for(gathered.at[pl.ds(0, 2 * TAPS - 1)], recv_sem.at[12])
         wait_for(gathered.at[pl.ds(0, XH * ZS - 1)], send_sem.at[12])
         wait_for(z_tx.at[pl.ds(0, TAPS - 1)], send_sem.at[10])
 
-    @pl.when(z >= TAPS)
+    @pl.when(lax.rem(z, 4) == 3)
     def _():
         wait_for(gathered.at[pl.ds(0, 2 * TAPS)], recv_sem.at[12])
         wait_for(z_tx, send_sem.at[10])
@@ -477,6 +488,8 @@
             pltpu.VMEM((2, POS + 2 * PAD, 3 * C), BF16),
             pltpu.VMEM((POS, C), F32),
             pltpu.VMEM((POS, C), F32),
+            pltpu.VMEM((POS, C), F32),
+            pltpu.VMEM((POS, C), F32),
             pltpu.VMEM((2, 128, POS), BF16),
             pltpu.VMEM((128, POS), BF16),
             pltpu.VMEM((2, 128, POS), BF16),
@@ -505,7 +518,7 @@
             pltpu.SemaphoreType.DMA((13,)),
             pltpu.SemaphoreType.DMA((13,)),
             pltpu.SemaphoreType.DMA((CHUNKS,)),
-            pltpu.SemaphoreType.REGULAR((3,)),
+            pltpu.SemaphoreType.REGULAR((4,)),
         ],
         compiler_params=pltpu.CompilerParams(
             collective_id=0, has_side_effects=True, vmem_limit_bytes=VMEM_BYTES

time: 61.9 us -> 55.1 us (0.89)
  Pallas kernels: 61.1 us -> 53.9 us
    pallas_call x1, Pallas kernels: 59.2 us -> 52 us  [per_device(): pl.pallas_call(kernel, name='video_block', out_shape=(jax.ShapeDtypeStruc...]
where the time goes in v3:
time: 55.1 us; the launch traced here: 54.5 us
  Pallas kernels  53.9 us (98%)
  between operations  0.64 us (1%)
    pallas_call x1, Pallas kernels, per_device(): pl.pallas_call(kernel, name='video_block', out_shape=(jax.ShapeDtypeStruc...  52 us
    pallas_call x1, Pallas kernels, per_device(): pl.pallas_call(write_out, name='write_out', out_shape=(jax.ShapeDtypeStru...  1.89 us

profile of v3, /device:TPU:1, one launch (start us, length us, event | category | flops | bytes accessed | tf_op | source)
XLA Modules:
  0.0 54.5 jit_solution(34701094112103292)
XLA Ops:
  0.6 52.0 %video_block.1 = (bf16[512,256]{1,0:T(8,128)(2,1)}, bf16[512,256]{1,0:T(8,128)(2,1)}, bf16[12,16,256]{2,1,0:T(8,128)(2,1)}) custom-call(bf16[512,256]{1,0:T(8,128)(2,1)} %bitcast.9, bf16[512,256]{1,0:T(8,128)(2,1)} %bitcast.10, f32[1,256]{1,0:T(1,128)} %bitcast.11, f32[1,256]{1,0:T(1,128)} %bitcast.12, bf16[3,768,256]{2,1,0:T(8,128)(2,1)} %bitcast.8, ...), custom_call_target="tpu_custom_call" | custom-call | tf_op jit(solution)/shard_map/video_block/pallas_call | solution.py:470
  52.6 1.9 %write_out.1 = (bf16[512,256]{1,0:T(8,128)(2,1)}, bf16[512,256]{1,0:T(8,128)(2,1)}, bf16[9,16,256]{2,1,0:T(8,128)(2,1)}, bf16[3,16,256]{2,1,0:T(8,128)(2,1)}) custom-call(bf16[512,256]{1,0:T(8,128)(2,1)} %get-tuple-element.11.result, bf16[512,256]{1,0:T(8,128)(2,1)} %get-tuple-element.12.grad, bf16[12,16,256]{2,1,0:T(8,128)(2,1)} %get-tuple-element.13.taps), custom_call_target="tpu_custom_call" | custom-call | tf_op jit(solution)/shard_map/write_out/pallas_call | solution.py:534

commit v4 on v3

--- a/solution.py
+++ b/solution.py
@@ -26,13 +26,14 @@
 )
 
 PLANE_ORDER = (
-    (2, 2), (1, 0), (0, 1), (2, 1), (0, 3), (3, 0), (1, 2), (1, 1),
-    (2, 3), (3, 3), (3, 2), (0, 2), (2, 0), (3, 1), (1, 3),
+    (2, 2), (2, 1), (1, 2), (2, 3), (3, 2), (1, 1), (3, 3), (1, 3),
+    (3, 1), (2, 0), (0, 2), (1, 0), (0, 1), (3, 0), (0, 3),
 )
 CHUNKS = 4
 PIECE = POS // CHUNKS
 
 ZS, XH, CHIPS = 16, 2, 8
+HALF = ZS // 2
 FRAMES = 2 * CHIPS
 
 
@@ -63,10 +64,6 @@
     lax.fori_loop(0, count, step, 0)
 
 
-def far_first(i):
-    return ZS // 2 + ((i + 1) // 2) * (1 - 2 * lax.rem(i, 2))
-
-
 def group_spread(row):
     lane = lax.broadcasted_iota(jnp.int32, row.shape, 1)
     for bit in (1, 2, 4):
@@ -96,9 +93,9 @@
     clips, cot, gain_in, shift_in, w_space, w_time,
     result_out, grad_out, taps_out,
     clips_v, cot4, w_space_v, w_time_v, w_space_t, w_time_t,
-    hcat, mgcat, act_s, hid_s, hid_grad_s, ng_s, h_t, h_tx, m_t, m_tx, mixed_own, mixed_halo, mixed_sib,
+    hcat, mgcat, act_s, hid_grad_s, ng_s, h_t, h_tx, m_t, m_tx, mixed_own, mixed_halo, mixed_sib,
     stat_tx, stat_rx, mean_tx, mean_rx,
-    rs_tx_a, rs_rx_a, rs_tx_b, rs_rx_b, z_tx, z_rx, fin_tx, gathered,
+    rs_tx_a, rs_rx_a, rs_tx_b, rs_rx_b, rs_tx_c, rs_rx_c, z_tx, z_rx, fin_tx, gathered,
     gain, shift, result_v, grad_v, taps_v, local_sem, send_sem, recv_sem, piece_sem, known,
 ):
     clip = lax.axis_index("clip")
@@ -211,71 +208,12 @@
     act = normed * gain[...] + shift[...]
     act_s[...] = act
     hidden = act / (1.0 + jnp.exp(-act))
-    hid_s[...] = hidden
     even, odd = by_parity(hidden.astype(BF16).T)
     first = core == 0
     h_tx[...] = jnp.where(first, odd, even)
     h_t[core] = jnp.where(first, even, odd)
     remote(h_tx, h_t.at[core], send_sem.at[3], recv_sem.at[3], clip, sibling).start()
 
-    for n in range(CHUNKS):
-        rows = pl.ds(n * PIECE, PIECE)
-        wait_for(cot4.at[2 + core, rows], piece_sem.at[n])
-        remote(
-            cot4.at[2 + core, rows], cot4.at[2 + core, rows],
-            send_sem.at[4], recv_sem.at[4], clip, sibling,
-        ).start()
-
-    copies[3].wait()
-    wait_for(cot4.at[0], recv_sem.at[2])
-    ng_s[...] = dot(cot4[0], w_time_t[0]) + dot(cot4[1], w_time_t[1])
-    hid_grad_s[...] = dot(cot4[1], w_time_t[0])
-    wait_for(cot4.at[0], recv_sem.at[4])
-    wait_for(cot4.at[0], send_sem.at[4])
-
-    @pl.when(q == CHIPS - 1)
-    def _():
-        cot4[2] = jnp.zeros((POS, C), BF16)
-        cot4[3] = jnp.zeros((POS, C), BF16)
-
-    for a in range(2):
-        if a == 0:
-            mg = ng_s[...] + dot(cot4[2], w_time_t[2])
-        else:
-            mg = hid_grad_s[...] + dot(cot4[2], w_time_t[1]) + dot(cot4[3], w_time_t[2])
-        mg = mg.astype(BF16).astype(F32)
-        for j in range(3):
-            mgcat[a, PAD : PAD + POS, j * C : (j + 1) * C] = shifted(mg, 1 - j, column).astype(BF16)
-
-    pl.semaphore_wait(known.at[0], 2)
-    tell(1)
-
-    wait_for(h_t.at[0], recv_sem.at[3])
-    for p in range(3):
-        rows = pl.ds((2 - p) * COLS, POS)
-        total = dot(h_t[0], mgcat[0, rows, :]) + dot(h_t[1], mgcat[1, rows, :])
-        total = total.astype(BF16)
-        for half in range(2):
-            for to in range(CHIPS):
-                for j in range(3):
-                    rs_tx_a[half * CHIPS + to, 3 * p + j] = total[
-                        to * 16 : to * 16 + 16, j * C + half * 128 : j * C + half * 128 + 128
-                    ]
-
-    def scatter(tx, rx, n):
-        for i, (by_x, by_y) in enumerate(PLANE_ORDER):
-            x = lax.rem(2 * xh + lax.rem(q, 2) + by_x, 2 * XH)
-            y = lax.rem(q // 2 + by_y, CHIPS // 2)
-            xh_to, q_to = x // 2, 2 * y + lax.rem(x, 2)
-            remote(
-                tx.at[xh_to * CHIPS + q_to], rx.at[i], send_sem.at[n], recv_sem.at[n],
-                xh_to * ZS + z, 2 * q_to + core,
-            ).start()
-
-    pl.semaphore_wait(known.at[3], 1)
-    scatter(rs_tx_a, rs_rx_a, 6)
-
-    hidden = hid_s[...]
     for j in range(3):
         hcat[PAD : PAD + POS, j * C : (j + 1) * C] = shifted(hidden, j - 1, column).astype(BF16)
     mixed = dot(hcat[0:POS, :], w_space_v[0])
@@ -288,6 +226,38 @@
     m_t[core] = jnp.where(first, even, odd)
     remote(m_tx, m_t.at[core], send_sem.at[5], recv_sem.at[5], clip, sibling).start()
 
+    for n in range(CHUNKS):
+        rows = pl.ds(n * PIECE, PIECE)
+        wait_for(cot4.at[2 + core, rows], piece_sem.at[n])
+        remote(
+            cot4.at[2 + core, rows], cot4.at[2 + core, rows],
+            send_sem.at[4], recv_sem.at[4], clip, sibling,
+        ).start()
+
+    copies[3].wait()
+    wait_for(cot4.at[0], recv_sem.at[2])
+    ng_s[...] = dot(cot4[0], w_time_t[0]) + dot(cot4[1], w_time_t[1])
+    hid_grad_s[...] = dot(cot4[1], w_time_t[0])
+    wait_for(cot4.at[0], recv_sem.at[4])
+    wait_for(cot4.at[0], send_sem.at[4])
+
+    @pl.when(q == CHIPS - 1)
+    def _():
+        cot4[2] = jnp.zeros((POS, C), BF16)
+        cot4[3] = jnp.zeros((POS, C), BF16)
+
+    def scatter(tx, rx, n):
+        for i, (by_x, by_y) in enumerate(PLANE_ORDER):
+            x = lax.rem(2 * xh + lax.rem(q, 2) + by_x, 2 * XH)
+            y = lax.rem(q // 2 + by_y, CHIPS // 2)
+            xh_to, q_to = x // 2, 2 * y + lax.rem(x, 2)
+            remote(
+                tx.at[xh_to * CHIPS + q_to], rx.at[i], send_sem.at[n], recv_sem.at[n],
+                xh_to * ZS + z, 2 * q_to + core,
+            ).start()
+
+    pl.semaphore_wait(known.at[0], 2)
+    tell(1)
     wait_for(m_t.at[0], recv_sem.at[5])
     for k in range(3):
         total = (dot(m_t[0], cot4[k]) + dot(m_t[1], cot4[k + 1])).astype(BF16)
@@ -297,7 +267,36 @@
                     to * 16 : to * 16 + 16, half * 128 : half * 128 + 128
                 ]
 
+    pl.semaphore_wait(known.at[3], 1)
     scatter(rs_tx_b, rs_rx_b, 7)
+
+    for a in range(2):
+        if a == 0:
+            mg = ng_s[...] + dot(cot4[2], w_time_t[2])
+        else:
+            mg = hid_grad_s[...] + dot(cot4[2], w_time_t[1]) + dot(cot4[3], w_time_t[2])
+        mg = mg.astype(BF16).astype(F32)
+        for j in range(3):
+            mgcat[a, PAD : PAD + POS, j * C : (j + 1) * C] = shifted(mg, 1 - j, column).astype(BF16)
+
+    wait_for(h_t.at[0], recv_sem.at[3])
+    for p in range(3):
+        rows = pl.ds((2 - p) * COLS, POS)
+        total = dot(h_t[0], mgcat[0, rows, :]) + dot(h_t[1], mgcat[1, rows, :])
+        total = total.astype(BF16)
+        for half in range(2):
+            for to in range(CHIPS):
+                for j in range(3):
+                    block = total[
+                        to * 16 : to * 16 + 16, j * C + half * 128 : j * C + half * 128 + 128
+                    ]
+                    if p < 2:
+                        rs_tx_a[half * CHIPS + to, 3 * p + j] = block
+                    else:
+                        rs_tx_c[half * CHIPS + to, j] = block
+        if p == 1:
+            scatter(rs_tx_a, rs_rx_a, 6)
+    scatter(rs_tx_c, rs_rx_c, 13)
     pl.semaphore_wait(known.at[1], 2)
     tell(2)
 
@@ -318,36 +317,34 @@
 
     me = xh * CHIPS + q
 
-    def along_z(lowest, highest):
-        def send(i):
-            to = lax.rem(z + far_first(i), ZS)
-
-            tap = to - to // 4
-
-            @pl.when((lax.rem(to, 4) < 3) & (tap >= lowest) & (tap < highest))
-            def _():
-                remote(
-                    z_tx.at[tap], z_rx.at[ZS - 1 - far_first(i)],
-                    send_sem.at[10], recv_sem.at[10], xh * ZS + to, frame,
-                ).start()
-
-        loop(ZS - 1, send)
-
-    wait_for(rs_rx_a, recv_sem.at[6])
-    for k in range(9):
-        total = rs_tx_a[me, k].astype(F32)
-        for i in range(XH * CHIPS - 1):
-            total = total + rs_rx_a[i, k].astype(F32)
-        z_tx[k] = total
+    def along_z(first_tap, count):
+        for tap in range(first_tap, first_tap + count):
+            for half in range(2):
+                to = tap % HALF + HALF * half
+
+                @pl.when(to != z)
+                def _(tap=tap, to=to):
+                    n = tap // HALF
+                    remote(
+                        z_tx.at[tap], z_rx.at[n * ZS + z], send_sem.at[10], recv_sem.at[10 + 4 * n],
+                        xh * ZS + to, frame,
+                    ).start()
+
+    def plane_sums(tx, rx, n, first_tap, count):
+        wait_for(rx, recv_sem.at[n])
+        for k in range(count):
+            total = tx[me, k].astype(F32)
+            for i in range(XH * CHIPS - 1):
+                total = total + rx[i, k].astype(F32)
+            z_tx[first_tap + k] = total
+
+    plane_sums(rs_tx_b, rs_rx_b, 7, 9, 3)
     pl.semaphore_wait(known.at[2], 2)
-    along_z(0, 9)
-    wait_for(rs_rx_b, recv_sem.at[7])
-    for k in range(3):
-        total = rs_tx_b[me, k].astype(F32)
-        for i in range(XH * CHIPS - 1):
-            total = total + rs_rx_b[i, k].astype(F32)
-        z_tx[9 + k] = total
-    along_z(9, TAPS)
+    along_z(9, 3)
+    plane_sums(rs_tx_a, rs_rx_a, 6, 0, 6)
+    along_z(0, 6)
+    plane_sums(rs_tx_c, rs_rx_c, 13, 6, 3)
+    along_z(6, 3)
 
     remote(mixed_own, mixed_halo, send_sem.at[8], recv_sem.at[8], clip, after).start()
 
@@ -365,30 +362,36 @@
     grad_copy.start()
 
     scale = 1.0 / math.sqrt(XH * ZS * FRAMES * POS)
-
-    @pl.when(lax.rem(z, 4) < 3)
-    def _():
-        wait_for(z_rx, recv_sem.at[10])
-        tap = z - z // 4
-        total = z_tx[tap]
-        for i in range(ZS - 1):
-            total = total + z_rx[i]
+    rest = lax.rem(z, HALF)
+
+    def finish(n):
+        tap = rest + HALF * n
+        wait_for(z_rx.at[pl.ds(0, ZS - 1)], recv_sem.at[10 + 4 * n])
+        z_rx[n * ZS + z] = z_tx[tap]
+        total = z_rx[n * ZS]
+        for i in range(1, ZS):
+            total = total + z_rx[n * ZS + i]
         done = (total * scale).astype(BF16)
-        fin_tx[...] = done
+        fin_tx[n] = done
         gathered[tap * 2 + xh] = done
 
         def hand(clip_to):
             remote(
-                fin_tx, gathered.at[tap * 2 + xh], send_sem.at[12], recv_sem.at[12], clip_to, frame
+                fin_tx.at[n], gathered.at[tap * 2 + xh], send_sem.at[12], recv_sem.at[12],
+                clip_to, frame,
             ).start()
 
-        def hand_out(i):
-            to = lax.rem(z + far_first(i), ZS)
+        for step in (-4, 3, -3, 2, -2, 1, -1):
+            to = lax.rem(z + step + ZS, ZS)
             hand((1 - xh) * ZS + to)
             hand(xh * ZS + to)
-
-        loop(ZS - 1, hand_out)
-        hand((1 - xh) * ZS + z)
+        hand(other)
+
+    @pl.when(rest < TAPS - HALF)
+    def _():
+        finish(1)
+
+    finish(0)
 
     wait_for(mixed_halo, recv_sem.at[8])
 
@@ -408,16 +411,17 @@
     result_copy = pltpu.make_async_copy(result_v, result_out, local_sem.at[7])
     result_copy.start()
 
-    @pl.when(lax.rem(z, 4) < 3)
+    @pl.when(rest < TAPS - HALF)
+    def _():
+        wait_for(gathered.at[pl.ds(0, 2 * TAPS - 2)], recv_sem.at[12])
+        wait_for(gathered.at[pl.ds(0, 2 * (ZS - 1))], send_sem.at[12])
+        wait_for(z_rx.at[pl.ds(0, 2 * TAPS - 2)], send_sem.at[10])
+
+    @pl.when(rest >= TAPS - HALF)
     def _():
         wait_for(gathered.at[pl.ds(0, 2 * TAPS - 1)], recv_sem.at[12])
-        wait_for(gathered.at[pl.ds(0, XH * ZS - 1)], send_sem.at[12])
-        wait_for(z_tx.at[pl.ds(0, TAPS - 1)], send_sem.at[10])
-
-    @pl.when(lax.rem(z, 4) == 3)
-    def _():
-        wait_for(gathered.at[pl.ds(0, 2 * TAPS)], recv_sem.at[12])
-        wait_for(z_tx, send_sem.at[10])
+        wait_for(gathered.at[pl.ds(0, ZS - 1)], send_sem.at[12])
+        wait_for(z_rx.at[pl.ds(0, 2 * TAPS - 1)], send_sem.at[10])
 
     for k in range(TAPS):
         for half in range(2):
@@ -432,6 +436,7 @@
     wait_for(m_tx, send_sem.at[5])
     wait_for(rs_rx_a, send_sem.at[6])
     wait_for(rs_rx_b, send_sem.at[7])
+    wait_for(rs_rx_c, send_sem.at[13])
     wait_for(mixed_own, send_sem.at[8])
     wait_for(mean_rx, send_sem.at[9])
     wait_for(mixed_own, send_sem.at[11])
@@ -489,7 +494,6 @@
             pltpu.VMEM((POS, C), F32),
             pltpu.VMEM((POS, C), F32),
             pltpu.VMEM((POS, C), F32),
-            pltpu.VMEM((POS, C), F32),
             pltpu.VMEM((2, 128, POS), BF16),
             pltpu.VMEM((128, POS), BF16),
             pltpu.VMEM((2, 128, POS), BF16),
@@ -501,13 +505,15 @@
             pltpu.VMEM((FRAMES - 1, 1, 2 * C), F32),
             pltpu.VMEM((1, 2 * C), F32),
             pltpu.VMEM((FRAMES - 1, 1, 2 * C), F32),
-            pltpu.VMEM((XH * CHIPS, 9, 16, 128), BF16),
-            pltpu.VMEM((XH * CHIPS - 1, 9, 16, 128), BF16),
+            pltpu.VMEM((XH * CHIPS, 6, 16, 128), BF16),
+            pltpu.VMEM((XH * CHIPS - 1, 6, 16, 128), BF16),
+            pltpu.VMEM((XH * CHIPS, 3, 16, 128), BF16),
+            pltpu.VMEM((XH * CHIPS - 1, 3, 16, 128), BF16),
             pltpu.VMEM((XH * CHIPS, 3, 16, 128), BF16),
             pltpu.VMEM((XH * CHIPS - 1, 3, 16, 128), BF16),
             pltpu.VMEM((TAPS, 16, 128), F32),
-            pltpu.VMEM((ZS - 1, 16, 128), F32),
-            pltpu.VMEM((16, 128), BF16),
+            pltpu.VMEM((2 * ZS, 16, 128), F32),
+            pltpu.VMEM((2, 16, 128), BF16),
             pltpu.VMEM((XH * ZS - 1, 16, 128), BF16),
             pltpu.VMEM((1, C), F32),
             pltpu.VMEM((1, C), F32),
@@ -515,8 +521,8 @@
             pltpu.VMEM((POS, C), BF16),
             pltpu.VMEM((TAPS, 16, C), BF16),
             pltpu.SemaphoreType.DMA((9,)),
-            pltpu.SemaphoreType.DMA((13,)),
-            pltpu.SemaphoreType.DMA((13,)),
+            pltpu.SemaphoreType.DMA((15,)),
+            pltpu.SemaphoreType.DMA((15,)),
             pltpu.SemaphoreType.DMA((CHUNKS,)),
             pltpu.SemaphoreType.REGULAR((4,)),
         ],

time: 55.1 us -> 54.1 us (0.982)
  the two profiles are of different devices: /device:TPU:1 before, /device:TPU:2 now
where the time goes in v4:
time: 54.1 us; the launch traced here: 53.9 us
  Pallas kernels  53.3 us (99%)
  between operations  0.64 us (1%)
    pallas_call x1, Pallas kernels, per_device(): pl.pallas_call(kernel, name='video_block', out_shape=(jax.ShapeDtypeStruc...  51.4 us
    pallas_call x1, Pallas kernels, per_device(): pl.pallas_call(write_out, name='write_out', out_shape=(jax.ShapeDtypeStru...  1.89 us

profile of v4, /device:TPU:2, one launch (start us, length us, event | category | flops | bytes accessed | tf_op | source)
XLA Modules:
  0.0 53.9 jit_solution(7492587390279512189)
XLA Ops:
  0.6 51.4 %video_block.1 = (bf16[512,256]{1,0:T(8,128)(2,1)}, bf16[512,256]{1,0:T(8,128)(2,1)}, bf16[12,16,256]{2,1,0:T(8,128)(2,1)}) custom-call(bf16[512,256]{1,0:T(8,128)(2,1)} %bitcast.9, bf16[512,256]{1,0:T(8,128)(2,1)} %bitcast.10, f32[1,256]{1,0:T(1,128)} %bitcast.11, f32[1,256]{1,0:T(1,128)} %bitcast.12, bf16[3,768,256]{2,1,0:T(8,128)(2,1)} %bitcast.8, ...), custom_call_target="tpu_custom_call" | custom-call | tf_op jit(solution)/shard_map/video_block/pallas_call | solution.py:475
  52.0 1.9 %write_out.1 = (bf16[512,256]{1,0:T(8,128)(2,1)}, bf16[512,256]{1,0:T(8,128)(2,1)}, bf16[9,16,256]{2,1,0:T(8,128)(2,1)}, bf16[3,16,256]{2,1,0:T(8,128)(2,1)}) custom-call(bf16[512,256]{1,0:T(8,128)(2,1)} %get-tuple-element.11.result, bf16[512,256]{1,0:T(8,128)(2,1)} %get-tuple-element.12.grad, bf16[12,16,256]{2,1,0:T(8,128)(2,1)} %get-tuple-element.13.taps), custom_call_target="tpu_custom_call" | custom-call | tf_op jit(solution)/shard_map/write_out/pallas_call | solution.py:540

commit v5 on v4

--- a/solution.py
+++ b/solution.py
@@ -64,6 +64,10 @@
     lax.fori_loop(0, count, step, 0)
 
 
+def far_first(i):
+    return (HALF - (i + 1) // 2) * (1 - 2 * lax.rem(i + 1, 2))
+
+
 def group_spread(row):
     lane = lax.broadcasted_iota(jnp.int32, row.shape, 1)
     for bit in (1, 2, 4):
@@ -95,7 +99,7 @@
     clips_v, cot4, w_space_v, w_time_v, w_space_t, w_time_t,
     hcat, mgcat, act_s, hid_grad_s, ng_s, h_t, h_tx, m_t, m_tx, mixed_own, mixed_halo, mixed_sib,
     stat_tx, stat_rx, mean_tx, mean_rx,
-    rs_tx_a, rs_rx_a, rs_tx_b, rs_rx_b, rs_tx_c, rs_rx_c, z_tx, z_rx, fin_tx, gathered,
+    rs_tx_a, rs_rx_a, rs_tx_b, rs_rx_b, rs_tx_c, rs_rx_c, rs_tx_d, rs_rx_d, z_tx, z_rx, fin_tx, gathered,
     gain, shift, result_v, grad_v, taps_v, local_sem, send_sem, recv_sem, piece_sem, known,
 ):
     clip = lax.axis_index("clip")
@@ -280,23 +284,18 @@
             mgcat[a, PAD : PAD + POS, j * C : (j + 1) * C] = shifted(mg, 1 - j, column).astype(BF16)
 
     wait_for(h_t.at[0], recv_sem.at[3])
-    for p in range(3):
+    row_groups = ((rs_tx_a, rs_rx_a, 6), (rs_tx_c, rs_rx_c, 13), (rs_tx_d, rs_rx_d, 15))
+    for p, (tx, rx, n) in enumerate(row_groups):
         rows = pl.ds((2 - p) * COLS, POS)
         total = dot(h_t[0], mgcat[0, rows, :]) + dot(h_t[1], mgcat[1, rows, :])
         total = total.astype(BF16)
         for half in range(2):
             for to in range(CHIPS):
                 for j in range(3):
-                    block = total[
+                    tx[half * CHIPS + to, j] = total[
                         to * 16 : to * 16 + 16, j * C + half * 128 : j * C + half * 128 + 128
                     ]
-                    if p < 2:
-                        rs_tx_a[half * CHIPS + to, 3 * p + j] = block
-                    else:
-                        rs_tx_c[half * CHIPS + to, j] = block
-        if p == 1:
-            scatter(rs_tx_a, rs_rx_a, 6)
-    scatter(rs_tx_c, rs_rx_c, 13)
+        scatter(tx, rx, n)
     pl.semaphore_wait(known.at[1], 2)
     tell(2)
 
@@ -318,17 +317,19 @@
     me = xh * CHIPS + q
 
     def along_z(first_tap, count):
-        for tap in range(first_tap, first_tap + count):
-            for half in range(2):
-                to = tap % HALF + HALF * half
-
-                @pl.when(to != z)
-                def _(tap=tap, to=to):
-                    n = tap // HALF
+        def send(i):
+            to = lax.rem(z + ZS + far_first(i), ZS)
+            for n in range(2):
+                tap = lax.rem(to, HALF) + HALF * n
+
+                @pl.when((tap >= first_tap) & (tap < first_tap + count))
+                def _(n=n, tap=tap):
                     remote(
                         z_tx.at[tap], z_rx.at[n * ZS + z], send_sem.at[10], recv_sem.at[10 + 4 * n],
                         xh * ZS + to, frame,
                     ).start()
+
+        loop(ZS - 1, send)
 
     def plane_sums(tx, rx, n, first_tap, count):
         wait_for(rx, recv_sem.at[n])
@@ -341,10 +342,9 @@
     plane_sums(rs_tx_b, rs_rx_b, 7, 9, 3)
     pl.semaphore_wait(known.at[2], 2)
     along_z(9, 3)
-    plane_sums(rs_tx_a, rs_rx_a, 6, 0, 6)
-    along_z(0, 6)
-    plane_sums(rs_tx_c, rs_rx_c, 13, 6, 3)
-    along_z(6, 3)
+    for p, (tx, rx, n) in enumerate(row_groups):
+        plane_sums(tx, rx, n, 3 * p, 3)
+        along_z(3 * p, 3)
 
     remote(mixed_own, mixed_halo, send_sem.at[8], recv_sem.at[8], clip, after).start()
 
@@ -437,6 +437,7 @@
     wait_for(rs_rx_a, send_sem.at[6])
     wait_for(rs_rx_b, send_sem.at[7])
     wait_for(rs_rx_c, send_sem.at[13])
+    wait_for(rs_rx_d, send_sem.at[15])
     wait_for(mixed_own, send_sem.at[8])
     wait_for(mean_rx, send_sem.at[9])
     wait_for(mixed_own, send_sem.at[11])
@@ -505,8 +506,10 @@
             pltpu.VMEM((FRAMES - 1, 1, 2 * C), F32),
             pltpu.VMEM((1, 2 * C), F32),
             pltpu.VMEM((FRAMES - 1, 1, 2 * C), F32),
-            pltpu.VMEM((XH * CHIPS, 6, 16, 128), BF16),
-            pltpu.VMEM((XH * CHIPS - 1, 6, 16, 128), BF16),
+            pltpu.VMEM((XH * CHIPS, 3, 16, 128), BF16),
+            pltpu.VMEM((XH * CHIPS - 1, 3, 16, 128), BF16),
+            pltpu.VMEM((XH * CHIPS, 3, 16, 128), BF16),
+            pltpu.VMEM((XH * CHIPS - 1, 3, 16, 128), BF16),
             pltpu.VMEM((XH * CHIPS, 3, 16, 128), BF16),
             pltpu.VMEM((XH * CHIPS - 1, 3, 16, 128), BF16),
             pltpu.VMEM((XH * CHIPS, 3, 16, 128), BF16),
@@ -521,8 +524,8 @@
             pltpu.VMEM((POS, C), BF16),
             pltpu.VMEM((TAPS, 16, C), BF16),
             pltpu.SemaphoreType.DMA((9,)),
-            pltpu.SemaphoreType.DMA((15,)),
-            pltpu.SemaphoreType.DMA((15,)),
+            pltpu.SemaphoreType.DMA((16,)),
+            pltpu.SemaphoreType.DMA((16,)),
             pltpu.SemaphoreType.DMA((CHUNKS,)),
             pltpu.SemaphoreType.REGULAR((4,)),
         ],

time: 54.1 us -> 53.4 us (0.987)
  the two profiles are of different devices: /device:TPU:2 before, /device:TPU:1 now
where the time goes in v5:
time: 53.4 us; the launch traced here: 53.2 us
  Pallas kernels  52.6 us (99%)
  between operations  0.64 us (1%)
    pallas_call x1, Pallas kernels, per_device(): pl.pallas_call(kernel, name='video_block', out_shape=(jax.ShapeDtypeStruc...  50.7 us
    pallas_call x1, Pallas kernels, per_device(): pl.pallas_call(write_out, name='write_out', out_shape=(jax.ShapeDtypeStru...  1.89 us

profile of v5, /device:TPU:1, one launch (start us, length us, event | category | flops | bytes accessed | tf_op | source)
XLA Modules:
  0.0 53.2 jit_solution(11993326121040236594)
XLA Ops:
  0.6 50.7 %video_block.1 = (bf16[512,256]{1,0:T(8,128)(2,1)}, bf16[512,256]{1,0:T(8,128)(2,1)}, bf16[12,16,256]{2,1,0:T(8,128)(2,1)}) custom-call(bf16[512,256]{1,0:T(8,128)(2,1)} %bitcast.9, bf16[512,256]{1,0:T(8,128)(2,1)} %bitcast.10, f32[1,256]{1,0:T(1,128)} %bitcast.11, f32[1,256]{1,0:T(1,128)} %bitcast.12, bf16[3,768,256]{2,1,0:T(8,128)(2,1)} %bitcast.8, ...), custom_call_target="tpu_custom_call" | custom-call | tf_op jit(solution)/shard_map/video_block/pallas_call | solution.py:476
  51.3 1.9 %write_out.1 = (bf16[512,256]{1,0:T(8,128)(2,1)}, bf16[512,256]{1,0:T(8,128)(2,1)}, bf16[9,16,256]{2,1,0:T(8,128)(2,1)}, bf16[3,16,256]{2,1,0:T(8,128)(2,1)}) custom-call(bf16[512,256]{1,0:T(8,128)(2,1)} %get-tuple-element.11.result, bf16[512,256]{1,0:T(8,128)(2,1)} %get-tuple-element.12.grad, bf16[12,16,256]{2,1,0:T(8,128)(2,1)} %get-tuple-element.13.taps), custom_call_target="tpu_custom_call" | custom-call | tf_op jit(solution)/shard_map/write_out/pallas_call | solution.py:543

commit v6 on v5

--- a/solution.py
+++ b/solution.py
@@ -218,6 +218,17 @@
     h_t[core] = jnp.where(first, even, odd)
     remote(h_tx, h_t.at[core], send_sem.at[3], recv_sem.at[3], clip, sibling).start()
 
+    def pass_on(n):
+        rows = pl.ds(n * PIECE, PIECE)
+        wait_for(cot4.at[2 + core, rows], piece_sem.at[n])
+        remote(
+            cot4.at[2 + core, rows], cot4.at[2 + core, rows],
+            send_sem.at[4], recv_sem.at[4], clip, sibling,
+        ).start()
+
+    for n in range(CHUNKS // 2):
+        pass_on(n)
+
     for j in range(3):
         hcat[PAD : PAD + POS, j * C : (j + 1) * C] = shifted(hidden, j - 1, column).astype(BF16)
     mixed = dot(hcat[0:POS, :], w_space_v[0])
@@ -230,13 +241,8 @@
     m_t[core] = jnp.where(first, even, odd)
     remote(m_tx, m_t.at[core], send_sem.at[5], recv_sem.at[5], clip, sibling).start()
 
-    for n in range(CHUNKS):
-        rows = pl.ds(n * PIECE, PIECE)
-        wait_for(cot4.at[2 + core, rows], piece_sem.at[n])
-        remote(
-            cot4.at[2 + core, rows], cot4.at[2 + core, rows],
-            send_sem.at[4], recv_sem.at[4], clip, sibling,
-        ).start()
+    for n in range(CHUNKS // 2, CHUNKS):
+        pass_on(n)
 
     copies[3].wait()
     wait_for(cot4.at[0], recv_sem.at[2])
@@ -348,6 +354,38 @@
 
     remote(mixed_own, mixed_halo, send_sem.at[8], recv_sem.at[8], clip, after).start()
 
+    scale = 1.0 / math.sqrt(XH * ZS * FRAMES * POS)
+    rest = lax.rem(z, HALF)
+
+    def finish(n):
+        tap = rest + HALF * n
+        wait_for(z_rx.at[pl.ds(0, ZS - 1)], recv_sem.at[10 + 4 * n])
+        z_rx[n * ZS + z] = z_tx[tap]
+        total = z_rx[n * ZS]
+        for i in range(1, ZS):
+            total = total + z_rx[n * ZS + i]
+        done = (total * scale).astype(BF16)
+        fin_tx[n] = done
+        gathered[tap * 2 + xh] = done
+
+        def hand(clip_to):
+            remote(
+                fin_tx.at[n], gathered.at[tap * 2 + xh], send_sem.at[12], recv_sem.at[12],
+                clip_to, frame,
+            ).start()
+
+        for step in (-4, 3, -3, 2, -2, 1, -1):
+            to = lax.rem(z + step + ZS, ZS)
+            hand((1 - xh) * ZS + to)
+            hand(xh * ZS + to)
+        hand(other)
+
+    @pl.when(rest < TAPS - HALF)
+    def _():
+        finish(1)
+
+    finish(0)
+
     wait_for(mean_rx, recv_sem.at[9])
     both = mean_tx[...]
     for i in range(FRAMES - 1):
@@ -360,38 +398,6 @@
     ).astype(BF16)
     grad_copy = pltpu.make_async_copy(grad_v, grad_out, local_sem.at[6])
     grad_copy.start()
-
-    scale = 1.0 / math.sqrt(XH * ZS * FRAMES * POS)
-    rest = lax.rem(z, HALF)
-
-    def finish(n):
-        tap = rest + HALF * n
-        wait_for(z_rx.at[pl.ds(0, ZS - 1)], recv_sem.at[10 + 4 * n])
-        z_rx[n * ZS + z] = z_tx[tap]
-        total = z_rx[n * ZS]
-        for i in range(1, ZS):
-            total = total + z_rx[n * ZS + i]
-        done = (total * scale).astype(BF16)
-        fin_tx[n] = done
-        gathered[tap * 2 + xh] = done
-
-        def hand(clip_to):
-            remote(
-                fin_tx.at[n], gathered.at[tap * 2 + xh], send_sem.at[12], recv_sem.at[12],
-                clip_to, frame,
-            ).start()
-
-        for step in (-4, 3, -3, 2, -2, 1, -1):
-            to = lax.rem(z + step + ZS, ZS)
-            hand((1 - xh) * ZS + to)
-            hand(xh * ZS + to)
-        hand(other)
-
-    @pl.when(rest < TAPS - HALF)
-    def _():
-        finish(1)
-
-    finish(0)
 
     wait_for(mixed_halo, recv_sem.at[8])
 
@@ -448,11 +454,8 @@
 def write_out(result, grad, taps, result_out, grad_out, space_out, time_out, *scratch):
     result_v, grad_v, taps_v, in_sem, out_sem = scratch
     moves = [(taps, taps_v, ((0, 9, space_out), (9, 3, time_out)))]
-    half = POS // 2
     for source, held, target in ((result, result_v, result_out), (grad, grad_v, grad_out)):
-        for n in range(2):
-            rows = pl.ds(n * half, half)
-            moves.append((source.at[rows], held.at[rows], ((0, half, target.at[rows]),)))
+        moves.append((source, held, ((0, POS, target),)))
     into = [
         pltpu.make_async_copy(source, held, in_sem.at[n])
         for n, (source, held, _) in enumerate(moves)

time: 53.4 us -> 53.3 us (level)
  no operation moved by 1% of the time
where the time goes in v6:
time: 53.3 us; the launch traced here: 53.1 us
  Pallas kernels  52.5 us (98%)
  between operations  0.64 us (1%)
    pallas_call x1, Pallas kernels, per_device(): pl.pallas_call(kernel, name='video_block', out_shape=(jax.ShapeDtypeStruc...  50.6 us
    pallas_call x1, Pallas kernels, per_device(): pl.pallas_call(write_out, name='write_out', out_shape=(jax.ShapeDtypeStru...  1.89 us

profile of v6, /device:TPU:1, one launch (start us, length us, event | category | flops | bytes accessed | tf_op | source)
XLA Modules:
  0.0 53.1 jit_solution(3304160730265193295)
XLA Ops:
  0.6 50.6 %video_block.1 = (bf16[512,256]{1,0:T(8,128)(2,1)}, bf16[512,256]{1,0:T(8,128)(2,1)}, bf16[12,16,256]{2,1,0:T(8,128)(2,1)}) custom-call(bf16[512,256]{1,0:T(8,128)(2,1)} %bitcast.9, bf16[512,256]{1,0:T(8,128)(2,1)} %bitcast.10, f32[1,256]{1,0:T(1,128)} %bitcast.11, f32[1,256]{1,0:T(1,128)} %bitcast.12, bf16[3,768,256]{2,1,0:T(8,128)(2,1)} %bitcast.8, ...), custom_call_target="tpu_custom_call" | custom-call | tf_op jit(solution)/shard_map/video_block/pallas_call | solution.py:479
  51.2 1.9 %write_out.1 = (bf16[512,256]{1,0:T(8,128)(2,1)}, bf16[512,256]{1,0:T(8,128)(2,1)}, bf16[9,16,256]{2,1,0:T(8,128)(2,1)}, bf16[3,16,256]{2,1,0:T(8,128)(2,1)}) custom-call(bf16[512,256]{1,0:T(8,128)(2,1)} %get-tuple-element.11.result, bf16[512,256]{1,0:T(8,128)(2,1)} %get-tuple-element.12.grad, bf16[12,16,256]{2,1,0:T(8,128)(2,1)} %get-tuple-element.13.taps), custom_call_target="tpu_custom_call" | custom-call | tf_op jit(solution)/shard_map/write_out/pallas_call | solution.py:546
